TPU v7x, 32 devices: a whole 2x2x4 slice. The times are simulated.
32 devices in a mesh: gx: 8 (over z, y), gy: 4 (over x, core).
Axes of the slice: x: 2, y: 2, z: 4, core: 2. Of those that a mesh axis runs over, the one named last changes fastest.
Arguments:
- points: bfloat16 [256, 128, 512], P(('gx', 'gy')), may hold values from -6 to 6
- moved_to: int32 [2, 2, 256], P(None, None, ('gx', 'gy')), may hold values from 0 to 255, as said below
- gains: float32 [2, 2, 512], replicated, may hold values from 0.1 to 1.9
- w_qkv: bfloat16 [2, 512, 1536], replicated, may hold values from -4 to 4
- w_out: bfloat16 [2, 512, 512], replicated, may hold values from -0.25 to 0.25
- w_up: bfloat16 [2, 512, 2048], replicated, may hold values from -0.25 to 0.25
- w_down: bfloat16 [2, 2048, 512], replicated, may hold values from -0.125 to 0.125
Outputs:
- encoded: bfloat16 [256, 128, 512], P(('gx', 'gy'))
Inputs may be any that keep to these rules, and one draw needn't show every extreme that they name: Each moved_to[l, s] is a permutation of the 256 positions. The owner of position p is p // 8, with owner index = gx index * 4 + gy index. Section 0 keeps every brick's gy index, section 1 its gx index. From one owner at most 2 bricks go to any one owner in section 0 and at most 2 in section 1; in every layer, section and group some owner sends exactly that many to one owner.
All inputs are finite; a program needn't handle non-finite values.
Results may differ from a plain program's by a relative error of at most 0.018.
Values may be sent and summed in bfloat16 or wider, within the bound.
No kernel may reach another device: no remote copies, remote signals or barrier semaphores. Data moves between devices by JAX's collectives and lax.ppermute only.
A program may use at most 128 MiB of HBM per device.

v0:
```python
import math

import jax
import jax.numpy as jnp
from jax import lax
from jax.sharding import PartitionSpec as P

HEAD_DIM = 16
PATCH = 512
LAYERS = 2


def normalize(values, gain):
    values = values.astype(jnp.float32)
    center = values - jnp.mean(values, axis=1, keepdims=True)
    spread = jnp.mean(center * center, axis=1, keepdims=True)
    return center * lax.rsqrt(spread + 1e-05) * gain


def attend_patch(patch):
    width = patch.shape[1] // 3
    count = patch.shape[0]
    heads = width // HEAD_DIM
    block = min(8, heads)
    scale = 1.0 / math.sqrt(HEAD_DIM)
    query = patch[:, :width].reshape(count, heads, HEAD_DIM)
    keys = patch[:, width : 2 * width].reshape(count, heads, HEAD_DIM)
    values = patch[:, 2 * width :].reshape(count, heads, HEAD_DIM)
    pieces = []
    for first in range(0, heads, block):
        scores = (
            jnp.einsum(
                "qhd,khd->hqk",
                query[:, first : first + block],
                keys[:, first : first + block],
                preferred_element_type=jnp.float32,
            )
            * scale
        )
        peak = jnp.max(scores, axis=2, keepdims=True)
        weights = jnp.exp(scores - peak)
        probs = (weights / jnp.sum(weights, axis=2, keepdims=True)).astype(jnp.bfloat16)
        mixed = jnp.einsum(
            "hqk,khd->qhd",
            probs,
            values[:, first : first + block],
            preferred_element_type=jnp.float32,
        )
        pieces.append(mixed.reshape(count, block * HEAD_DIM))
    return jnp.concatenate(pieces, axis=1).astype(jnp.bfloat16)


def encoder_layer(bricks, gain, w_qkv, w_out, w_up, w_down):
    shape = bricks.shape
    flat = bricks.reshape(-1, shape[2])
    normed = normalize(flat, gain[0]).astype(jnp.bfloat16)
    projected = jnp.dot(normed, w_qkv, preferred_element_type=jnp.float32).astype(jnp.bfloat16)
    attended = lax.map(attend_patch, projected.reshape(-1, PATCH, projected.shape[1])).reshape(
        flat.shape
    )
    mixed = (
        flat.astype(jnp.float32) + jnp.dot(attended, w_out, preferred_element_type=jnp.float32)
    ).astype(jnp.bfloat16)
    inner = normalize(mixed, gain[1]).astype(jnp.bfloat16)
    hidden = jax.nn.gelu(
        jnp.dot(inner, w_up, preferred_element_type=jnp.float32), approximate=False
    ).astype(jnp.bfloat16)
    result = mixed.astype(jnp.float32) + jnp.dot(hidden, w_down, preferred_element_type=jnp.float32)
    return result.astype(jnp.bfloat16).reshape(shape)


def pack_slots(bricks, targets, places, peers):
    count = targets.shape[0]
    capacity = max(2, -(-count // peers))
    width = peers * capacity
    order = jnp.arange(count)
    before = (targets[:, None] == targets[None, :]) & (order[None, :] < order[:, None])
    rank = jnp.sum(before.astype(jnp.int32), axis=1)
    slot_id = targets * capacity + rank
    hit = slot_id[None, :] == jnp.arange(width)[:, None]
    source = jnp.sum(jnp.where(hit, order[None, :], 0), axis=1)
    tags = jnp.sum(jnp.where(hit, places[None, :] + 1, 0), axis=1).astype(jnp.bfloat16)
    return (jnp.take(bricks, source, axis=0), tags)


def arrival_order(tags, count):
    wanted = jnp.arange(1, count + 1).astype(jnp.float32)
    match = tags.astype(jnp.float32)[None, :] == wanted[:, None]
    return jnp.sum(jnp.where(match, jnp.arange(tags.shape[0])[None, :], 0), axis=1)


def per_device(points, moved_to, gains, w_qkv, w_out, w_up, w_down):
    bricks = points
    count = points.shape[0]
    rows_size = lax.axis_size("gx")
    column_size = lax.axis_size("gy")
    for layer in range(LAYERS):
        moved_row = moved_to[layer, 0]
        owner = moved_row // count
        outgoing, tags = pack_slots(bricks, owner // column_size, moved_row % count, rows_size)
        arrived, arrived_tags = (
            lax.all_to_all(outgoing, "gx", split_axis=0, concat_axis=0, tiled=True),
            lax.all_to_all(tags, "gx", split_axis=0, concat_axis=0, tiled=True),
        )
        bricks = jnp.take(arrived, arrival_order(arrived_tags, count), axis=0)
        moved_col = moved_to[layer, 1]
        column = moved_col // count % column_size
        places = moved_col % count
        outgoing, tags = pack_slots(bricks, column, places, column_size)
        arrived, arrived_tags = (
            lax.all_to_all(outgoing, "gy", split_axis=0, concat_axis=0, tiled=True),
            lax.all_to_all(tags, "gy", split_axis=0, concat_axis=0, tiled=True),
        )
        bricks = jnp.take(arrived, arrival_order(arrived_tags, count), axis=0)
        bricks = encoder_layer(
            bricks, gains[layer], w_qkv[layer], w_out[layer], w_up[layer], w_down[layer]
        )
    return bricks


def solution(mesh):
    placed = (P(("gx", "gy"), None, None), P(None, None, ("gx", "gy")), P(), P(), P(), P(), P())
    return jax.shard_map(
        per_device,
        mesh=mesh,
        in_specs=placed,
        out_specs=P(("gx", "gy"), None, None),
        check_vma=False,
    )
```

profile of v0, /device:TPU:13, one launch (start us, length us, event | category | flops | bytes accessed | tf_op | source)
XLA Modules:
  0.0 515.3 jit_solution(3517616739940899385)
XLA Ops:
  1.9 5.7 %all-to-all-start.1 = ((bf16[8,2,1]{1,2,0:T(2,128)(2,1)}), bf16[8,2,1]{1,2,0:T(2,128)(2,1)S(1)}, u32[]{:S(2)}, u32[]{:S(2)}) async-start(bf16[8,2,1]{1,2,0:T(2,128)(2,1)} %convert_element_type.286), calls=%async_computation.1 | async-start | bytes 8192 | tf_op jit(solution)/shard_map/all_to_all | solution.py:103
  10.8 5.3 %all-to-all-start.5 = ((bf16[8,2,1]{1,2,0:T(2,128)(2,1)}), bf16[8,2,1]{1,2,0:T(2,128)(2,1)S(1)}, u32[]{:S(2)}, u32[]{:S(2)}) async-start(bf16[8,2,1]{1,2,0:T(2,128)(2,1)} %convert_element_type.284), calls=%async_computation.5 | async-start | bytes 8192 | tf_op jit(solution)/shard_map/all_to_all | solution.py:103
  19.3 5.6 %all-to-all-start = ((bf16[16,128,512]{2,1,0:T(8,128)(2,1)}), bf16[16,128,512]{2,1,0:T(8,128)(2,1)S(1)}, u32[]{:S(2)}, u32[]{:S(2)}) async-start(bf16[16,128,512]{2,1,0:T(8,128)(2,1)} %broadcast_select_fusion.1), calls=%async_computation | async-start | bytes 4194304 | tf_op jit(solution)/shard_map/all_to_all | solution.py:102
  29.2 41.4 %all-to-all-done = bf16[16,128,512]{2,1,0:T(8,128)(2,1)S(1)} async-done(((bf16[16,128,512]{2,1,0:T(8,128)(2,1)}), bf16[16,128,512]{2,1,0:T(8,128)(2,1)S(1)}, u32[]{:S(2)}, u32[]{:S(2)}) %all-to-all-start) | async-done | bytes 2097184 | tf_op jit(solution)/shard_map/all_to_all | solution.py:102
  70.5 3.6 all-to-all-start.3
  77.1 6.2 %all_to_all.44 = bf16[4,2,1]{1,2,0:T(2,128)(2,1)S(1)} all-to-all(bf16[4,2,1]{1,2,0:T(2,128)(2,1)S(1)} %convert_element_type.283), channel_id=1, replica_groups=mesh['gx'=8,'gy'=4] {'gy'}, dimensions={0} | all-to-all | bytes 32 | tf_op jit(solution)/shard_map/all_to_all | solution.py:112
  83.3 4.2 all-to-all-start.2
  88.4 12.6 %all-to-all-done.2 = bf16[8,128,512]{2,1,0:T(8,128)(2,1)S(1)} async-done(((bf16[8,128,512]{2,1,0:T(8,128)(2,1)}), bf16[8,128,512]{2,1,0:T(8,128)(2,1)S(1)}, u32[]{:S(2)}, u32[]{:S(2)}) %all-to-all-start.2) | async-done | bytes 1048608 | tf_op jit(solution)/shard_map/all_to_all | solution.py:111
  103.0 5.0 convolution_convert_fusion.1
  109.0 135.7 %while.20 = (s32[]{:T(128)}, bf16[2,512,512]{2,1,0:T(8,128)(2,1)}, bf16[2,512,1536]{2,1,0:T(8,128)(2,1)}, s32[]{:T(128)}) while((s32[]{:T(128)}, bf16[2,512,512]{2,1,0:T(8,128)(2,1)}, bf16[2,512,1536]{2,1,0:T(8,128)(2,1)}, s32[]{:T(128)}) %tuple.84), condition=%wide.region_19.23_spmd, body=%wide.region_10.0_spmd.sunk | while | flops 614748160 | bytes 261226736 | solution.py:58
  109.5 2.7 constant_dynamic-slice_fusion.4
  115.3 3.2 copy-done.4
  118.5 2.2 fusion.412
  120.7 8.7 %fusion.413 = bf16[8,16,512]{2,1,0:T(8,128)(2,1)S(1)} fusion(bf16[512,32,16]{0,2,1:T(8,128)(2,1)S(1)} %bitcast.250, f32[8,512]{1,0:T(8,128)S(1)} %fusion.412, f32[8,512,512]{1,2,0:T(8,128)} %copy-done.4), kind=kOutput, calls=%fused_computation.39.clone.1 | convolution fusion | flops 77664768 | bytes 9060352 | tf_op jit(solution)/shard_map/while/body/eval_jaxpr/hqk,khd->qhd/dot_general | solution.py:43
  130.7 3.2 copy-done.6
  134.0 2.2 fusion.409
  136.1 8.7 %fusion.410 = bf16[8,16,512]{2,1,0:T(8,128)(2,1)S(1)} fusion(bf16[512,32,16]{0,2,1:T(8,128)(2,1)S(1)} %bitcast.251, f32[8,512]{1,0:T(8,128)S(1)} %fusion.409, f32[8,512,512]{1,2,0:T(8,128)} %copy-done.6), kind=kOutput, calls=%fused_computation.38.clone.1 | convolution fusion | flops 77664768 | bytes 9060352 | tf_op jit(solution)/shard_map/while/body/eval_jaxpr/hqk,khd->qhd/dot_general | solution.py:43
  146.2 3.2 copy-done.7
  149.4 2.2 fusion.406
  151.5 8.7 %fusion.407 = bf16[8,16,512]{2,1,0:T(8,128)(2,1)S(1)} fusion(bf16[512,32,16]{0,2,1:T(8,128)(2,1)S(1)} %bitcast.252, f32[8,512]{1,0:T(8,128)S(1)} %fusion.406, f32[8,512,512]{1,2,0:T(8,128)} %copy-done.7), kind=kOutput, calls=%fused_computation.37.clone.1 | convolution fusion | flops 77664768 | bytes 9060352 | tf_op jit(solution)/shard_map/while/body/eval_jaxpr/hqk,khd->qhd/dot_general | solution.py:43
  161.6 3.2 copy-done.2
  164.8 2.2 fusion.403
  167.0 8.8 %fusion.404 = bf16[8,16,512]{2,1,0:T(8,128)(2,1)S(1)} fusion(bf16[512,32,16]{0,2,1:T(8,128)(2,1)S(1)} %bitcast.253, f32[8,512]{1,0:T(8,128)S(1)} %fusion.403, f32[8,512,512]{1,2,0:T(8,128)} %copy-done.2), kind=kOutput, calls=%fused_computation.36.clone.1 | convolution fusion | flops 77664768 | bytes 9060352 | tf_op jit(solution)/shard_map/while/body/eval_jaxpr/hqk,khd->qhd/dot_general | solution.py:43
  177.1 2.7 constant_dynamic-slice_fusion.4
  182.9 3.2 copy-done.4
  186.1 2.2 fusion.412
  188.3 8.7 %fusion.413 = bf16[8,16,512]{2,1,0:T(8,128)(2,1)S(1)} fusion(bf16[512,32,16]{0,2,1:T(8,128)(2,1)S(1)} %bitcast.250, f32[8,512]{1,0:T(8,128)S(1)} %fusion.412, f32[8,512,512]{1,2,0:T(8,128)} %copy-done.4), kind=kOutput, calls=%fused_computation.39.clone.1 | convolution fusion | flops 77664768 | bytes 9060352 | tf_op jit(solution)/shard_map/while/body/eval_jaxpr/hqk,khd->qhd/dot_general | solution.py:43
  198.3 3.2 copy-done.6
  203.7 8.7 %fusion.410 = bf16[8,16,512]{2,1,0:T(8,128)(2,1)S(1)} fusion(bf16[512,32,16]{0,2,1:T(8,128)(2,1)S(1)} %bitcast.251, f32[8,512]{1,0:T(8,128)S(1)} %fusion.409, f32[8,512,512]{1,2,0:T(8,128)} %copy-done.6), kind=kOutput, calls=%fused_computation.38.clone.1 | convolution fusion | flops 77664768 | bytes 9060352 | tf_op jit(solution)/shard_map/while/body/eval_jaxpr/hqk,khd->qhd/dot_general | solution.py:43
  213.7 3.2 copy-done.7
  216.9 2.2 fusion.406
  219.1 8.7 %fusion.407 = bf16[8,16,512]{2,1,0:T(8,128)(2,1)S(1)} fusion(bf16[512,32,16]{0,2,1:T(8,128)(2,1)S(1)} %bitcast.252, f32[8,512]{1,0:T(8,128)S(1)} %fusion.406, f32[8,512,512]{1,2,0:T(8,128)} %copy-done.7), kind=kOutput, calls=%fused_computation.37.clone.1 | convolution fusion | flops 77664768 | bytes 9060352 | tf_op jit(solution)/shard_map/while/body/eval_jaxpr/hqk,khd->qhd/dot_general | solution.py:43
  229.1 3.2 copy-done.2
  234.5 8.8 %fusion.404 = bf16[8,16,512]{2,1,0:T(8,128)(2,1)S(1)} fusion(bf16[512,32,16]{0,2,1:T(8,128)(2,1)S(1)} %bitcast.253, f32[8,512]{1,0:T(8,128)S(1)} %fusion.403, f32[8,512,512]{1,2,0:T(8,128)} %copy-done.2), kind=kOutput, calls=%fused_computation.36.clone.1 | convolution fusion | flops 77664768 | bytes 9060352 | tf_op jit(solution)/shard_map/while/body/eval_jaxpr/hqk,khd->qhd/dot_general | solution.py:43
  244.8 2.5 convert_reduce_fusion.1
  247.8 22.2 %fusion.174 = bf16[1024,512]{1,0:T(8,128)(2,1)S(1)} fusion(bf16[1024,512]{1,0:T(8,128)(2,1)S(1)} %get-tuple-element.121, bf16[2,2048,512]{2,1,0:T(8,128)(2,1)} %param.23, bf16[2,512,2048]{2,1,0:T(8,128)(2,1)} %param.22, f32[512]{0:T(512)S(1)} %bitcast.274, f32[1024]{0:T(1024)S(1)} %add_rsqrt_fusion.2, f32[1024]{0:T(1024)S(1)} %broadcast_multiply_fusion.1), kind=kOutput, calls=%fused_computation.178 | convolution fusion | flops 4435476480 | bytes 7350272 | tf_op jit(solution)/shard_map/dot_general | solution.py:68
  272.6 6.9 %all-to-all-start.4 = ((bf16[16,128,512]{2,1,0:T(8,128)(2,1)}), bf16[16,128,512]{2,1,0:T(8,128)(2,1)S(1)}, u32[]{:S(2)}, u32[]{:S(2)}) async-start(bf16[16,128,512]{2,1,0:T(8,128)(2,1)} %broadcast_select_fusion), calls=%async_computation.4 | async-start | bytes 4194304 | tf_op jit(solution)/shard_map/all_to_all | solution.py:102
  279.6 45.6 %all-to-all-done.4 = bf16[16,128,512]{2,1,0:T(8,128)(2,1)S(1)} async-done(((bf16[16,128,512]{2,1,0:T(8,128)(2,1)}), bf16[16,128,512]{2,1,0:T(8,128)(2,1)S(1)}, u32[]{:S(2)}, u32[]{:S(2)}) %all-to-all-start.4) | async-done | bytes 2097184 | tf_op jit(solution)/shard_map/all_to_all | solution.py:102
  327.8 4.0 all-to-all-start.6
  331.8 13.6 %all-to-all-done.6 = bf16[8,128,512]{2,1,0:T(8,128)(2,1)S(1)} async-done(((bf16[8,128,512]{2,1,0:T(8,128)(2,1)}), bf16[8,128,512]{2,1,0:T(8,128)(2,1)S(1)}, u32[]{:S(2)}, u32[]{:S(2)}) %all-to-all-start.6) | async-done | bytes 1048608 | tf_op jit(solution)/shard_map/all_to_all | solution.py:111
  347.3 5.0 convolution_convert_fusion
  353.3 135.7 %while.21 = (s32[]{:T(128)}, bf16[2,512,512]{2,1,0:T(8,128)(2,1)}, bf16[2,512,1536]{2,1,0:T(8,128)(2,1)}, s32[]{:T(128)}) while((s32[]{:T(128)}, bf16[2,512,512]{2,1,0:T(8,128)(2,1)}, bf16[2,512,1536]{2,1,0:T(8,128)(2,1)}, s32[]{:T(128)}) %tuple.83), condition=%wide.region_41.45_spmd, body=%wide.region_32.44_spmd.sunk | while | flops 614748160 | bytes 261226736 | solution.py:58
  353.5 2.7 constant_dynamic-slice_fusion.5
  359.3 3.2 copy-done.5
  362.5 2.2 fusion.441
  364.7 8.7 %fusion.442 = bf16[8,16,512]{2,1,0:T(8,128)(2,1)S(1)} fusion(bf16[512,32,16]{0,2,1:T(8,128)(2,1)S(1)} %bitcast.254, f32[8,512]{1,0:T(8,128)S(1)} %fusion.441, f32[8,512,512]{1,2,0:T(8,128)} %copy-done.5), kind=kOutput, calls=%fused_computation.94.clone.1 | convolution fusion | flops 77664768 | bytes 9060352 | tf_op jit(solution)/shard_map/while/body/eval_jaxpr/hqk,khd->qhd/dot_general | solution.py:43
  374.7 3.2 copy-done.8
  378.0 2.2 fusion.438
  380.1 8.7 %fusion.439 = bf16[8,16,512]{2,1,0:T(8,128)(2,1)S(1)} fusion(bf16[512,32,16]{0,2,1:T(8,128)(2,1)S(1)} %bitcast.255, f32[8,512]{1,0:T(8,128)S(1)} %fusion.438, f32[8,512,512]{1,2,0:T(8,128)} %copy-done.8), kind=kOutput, calls=%fused_computation.93.clone.1 | convolution fusion | flops 77664768 | bytes 9060352 | tf_op jit(solution)/shard_map/while/body/eval_jaxpr/hqk,khd->qhd/dot_general | solution.py:43
  390.2 3.2 copy-done.9
  395.5 8.7 %fusion.436 = bf16[8,16,512]{2,1,0:T(8,128)(2,1)S(1)} fusion(bf16[512,32,16]{0,2,1:T(8,128)(2,1)S(1)} %bitcast.256, f32[8,512]{1,0:T(8,128)S(1)} %fusion.435, f32[8,512,512]{1,2,0:T(8,128)} %copy-done.9), kind=kOutput, calls=%fused_computation.92.clone.1 | convolution fusion | flops 77664768 | bytes 9060352 | tf_op jit(solution)/shard_map/while/body/eval_jaxpr/hqk,khd->qhd/dot_general | solution.py:43
  405.6 3.2 copy-done.3
  411.0 8.8 %fusion.433 = bf16[8,16,512]{2,1,0:T(8,128)(2,1)S(1)} fusion(bf16[512,32,16]{0,2,1:T(8,128)(2,1)S(1)} %bitcast.257, f32[8,512]{1,0:T(8,128)S(1)} %fusion.432, f32[8,512,512]{1,2,0:T(8,128)} %copy-done.3), kind=kOutput, calls=%fused_computation.91.clone.1 | convolution fusion | flops 77664768 | bytes 9060352 | tf_op jit(solution)/shard_map/while/body/eval_jaxpr/hqk,khd->qhd/dot_general | solution.py:43
  421.1 2.7 constant_dynamic-slice_fusion.5
  426.9 3.2 copy-done.5
  432.3 8.7 %fusion.442 = bf16[8,16,512]{2,1,0:T(8,128)(2,1)S(1)} fusion(bf16[512,32,16]{0,2,1:T(8,128)(2,1)S(1)} %bitcast.254, f32[8,512]{1,0:T(8,128)S(1)} %fusion.441, f32[8,512,512]{1,2,0:T(8,128)} %copy-done.5), kind=kOutput, calls=%fused_computation.94.clone.1 | convolution fusion | flops 77664768 | bytes 9060352 | tf_op jit(solution)/shard_map/while/body/eval_jaxpr/hqk,khd->qhd/dot_general | solution.py:43
  442.3 3.2 copy-done.8
  447.7 8.7 %fusion.439 = bf16[8,16,512]{2,1,0:T(8,128)(2,1)S(1)} fusion(bf16[512,32,16]{0,2,1:T(8,128)(2,1)S(1)} %bitcast.255, f32[8,512]{1,0:T(8,128)S(1)} %fusion.438, f32[8,512,512]{1,2,0:T(8,128)} %copy-done.8), kind=kOutput, calls=%fused_computation.93.clone.1 | convolution fusion | flops 77664768 | bytes 9060352 | tf_op jit(solution)/shard_map/while/body/eval_jaxpr/hqk,khd->qhd/dot_general | solution.py:43
  457.7 3.2 copy-done.9
  463.1 8.7 %fusion.436 = bf16[8,16,512]{2,1,0:T(8,128)(2,1)S(1)} fusion(bf16[512,32,16]{0,2,1:T(8,128)(2,1)S(1)} %bitcast.256, f32[8,512]{1,0:T(8,128)S(1)} %fusion.435, f32[8,512,512]{1,2,0:T(8,128)} %copy-done.9), kind=kOutput, calls=%fused_computation.92.clone.1 | convolution fusion | flops 77664768 | bytes 9060352 | tf_op jit(solution)/shard_map/while/body/eval_jaxpr/hqk,khd->qhd/dot_general | solution.py:43
  473.1 3.2 copy-done.3
  478.5 8.8 %fusion.433 = bf16[8,16,512]{2,1,0:T(8,128)(2,1)S(1)} fusion(bf16[512,32,16]{0,2,1:T(8,128)(2,1)S(1)} %bitcast.257, f32[8,512]{1,0:T(8,128)S(1)} %fusion.432, f32[8,512,512]{1,2,0:T(8,128)} %copy-done.3), kind=kOutput, calls=%fused_computation.91.clone.1 | convolution fusion | flops 77664768 | bytes 9060352 | tf_op jit(solution)/shard_map/while/body/eval_jaxpr/hqk,khd->qhd/dot_general | solution.py:43
  489.0 2.5 convert_reduce_fusion
  492.1 23.0 %fusion.175 = bf16[1024,512]{1,0:T(8,128)(2,1)} fusion(bf16[1024,512]{1,0:T(8,128)(2,1)S(1)} %get-tuple-element.123, bf16[2,2048,512]{2,1,0:T(8,128)(2,1)} %param.23, bf16[2,512,2048]{2,1,0:T(8,128)(2,1)} %param.22, f32[512]{0:T(512)S(1)} %bitcast.273, f32[1024]{0:T(1024)S(1)} %add_rsqrt_fusion, f32[1024]{0:T(1024)S(1)} %broadcast_multiply_fusion), kind=kOutput, calls=%fused_computation.179 | convolution fusion | flops 4435476480 | bytes 7350272 | tf_op jit(solution)/shard_map/dot_general | solution.py:68
  (192 shorter events, 78.9 us)
Async XLA Ops:
  0.0 8.6 %copy-start = (bf16[8,128,512]{2,1,0:T(8,128)(2,1)S(1)}, bf16[8,128,512]{2,1,0:T(8,128)(2,1)}, u32[]{:S(2)}) copy-start(bf16[8,128,512]{2,1,0:T(8,128)(2,1)} %param.17) | copy-start | bytes 3145732
  0.0 27.6 %copy-start.17 = (f32[2,2,512]{2,1,0:T(2,128)S(1)}, f32[2,2,512]{2,1,0:T(2,128)}, u32[]{:S(2)}) copy-start(f32[2,2,512]{2,1,0:T(2,128)} %param.19) | copy-start | bytes 24580
  1.9 8.9 %all-to-all-start.1 = ((bf16[8,2,1]{1,2,0:T(2,128)(2,1)}), bf16[8,2,1]{1,2,0:T(2,128)(2,1)S(1)}, u32[]{:S(2)}, u32[]{:S(2)}) async-start(bf16[8,2,1]{1,2,0:T(2,128)(2,1)} %convert_element_type.286), calls=%async_computation.1 | async-start | bytes 8192 | tf_op jit(solution)/shard_map/all_to_all | solution.py:103
  10.8 8.5 %all-to-all-start.5 = ((bf16[8,2,1]{1,2,0:T(2,128)(2,1)}), bf16[8,2,1]{1,2,0:T(2,128)(2,1)S(1)}, u32[]{:S(2)}, u32[]{:S(2)}) async-start(bf16[8,2,1]{1,2,0:T(2,128)(2,1)} %convert_element_type.284), calls=%async_computation.5 | async-start | bytes 8192 | tf_op jit(solution)/shard_map/all_to_all | solution.py:103
  19.3 51.3 %all-to-all-start = ((bf16[16,128,512]{2,1,0:T(8,128)(2,1)}), bf16[16,128,512]{2,1,0:T(8,128)(2,1)S(1)}, u32[]{:S(2)}, u32[]{:S(2)}) async-start(bf16[16,128,512]{2,1,0:T(8,128)(2,1)} %broadcast_select_fusion.1), calls=%async_computation | async-start | bytes 4194304 | tf_op jit(solution)/shard_map/all_to_all | solution.py:102
  70.5 6.5 %all-to-all-start.3 = ((bf16[4,2,1]{1,2,0:T(2,128)(2,1)}), bf16[4,2,1]{1,2,0:T(2,128)(2,1)S(1)}, u32[]{:S(2)}, u32[]{:S(2)}) async-start(bf16[4,2,1]{1,2,0:T(2,128)(2,1)} %convert_element_type.285), calls=%async_computation.3 | async-start | bytes 4096 | tf_op jit(solution)/shard_map/all_to_all | solution.py:112
  83.3 17.8 %all-to-all-start.2 = ((bf16[8,128,512]{2,1,0:T(8,128)(2,1)}), bf16[8,128,512]{2,1,0:T(8,128)(2,1)S(1)}, u32[]{:S(2)}, u32[]{:S(2)}) async-start(bf16[8,128,512]{2,1,0:T(8,128)(2,1)} %broadcast_select_fusion.6), calls=%async_computation.2 | async-start | bytes 2097152 | tf_op jit(solution)/shard_map/all_to_all | solution.py:111
  102.1 7.0 %copy-start.11 = (bf16[8,128,512]{2,1,0:T(8,128)(2,1)}, bf16[8,128,512]{2,1,0:T(8,128)(2,1)S(1)}, u32[]{:S(2)}) copy-start(bf16[8,128,512]{2,1,0:T(8,128)(2,1)S(1)} %get-tuple-element.95) | copy-start | bytes 3145732
  109.0 138.8 %copy-start.19 = (f32[1,1,512]{2,1,0:T(1,128)S(1)}, f32[1,1,512]{2,1,0:T(1,128)}, u32[]{:S(2)}) copy-start(f32[1,1,512]{2,1,0:T(1,128)} %get-tuple-element.111) | copy-start | bytes 6148
  115.3 3.2 copy-start.4
  130.7 3.2 copy-start.6
  146.1 3.2 copy-start.7
  161.6 3.2 copy-start.2
  167.0 9.1 %copy-start.14 = (bf16[2,512,512]{2,1,0:T(8,128)(2,1)S(1)}, bf16[2,512,512]{2,1,0:T(8,128)(2,1)}, u32[]{:S(2)}) copy-start(bf16[2,512,512]{2,1,0:T(8,128)(2,1)} %get-tuple-element.187) | copy-start | bytes 3145732 | tf_op jit(solution)/shard_map/while
  176.1 1.0 copy-start.15
  182.9 3.2 copy-start.4
  198.3 3.2 copy-start.6
  213.7 3.2 copy-start.7
  229.1 3.2 copy-start.2
  234.5 9.1 %copy-start.14 = (bf16[2,512,512]{2,1,0:T(8,128)(2,1)S(1)}, bf16[2,512,512]{2,1,0:T(8,128)(2,1)}, u32[]{:S(2)}) copy-start(bf16[2,512,512]{2,1,0:T(8,128)(2,1)} %get-tuple-element.187) | copy-start | bytes 3145732 | tf_op jit(solution)/shard_map/while
  243.7 1.0 copy-start.15
  247.8 23.2 %copy-start.20 = (pred[16]{0:T(512)(128)(4,1)S(1)}, pred[16]{0:T(512)(128)(4,1)}, u32[]{:S(2)}) copy-start(pred[16]{0:T(512)(128)(4,1)} %compare_and_fusion.3) | copy-start | bytes 52
  270.1 9.5 %copy-start.23 = (s32[8]{0:T(128)S(1)}, s32[8]{0:T(128)}, u32[]{:S(2)}) copy-start(s32[8]{0:T(128)} %get-tuple-element.71) | copy-start | bytes 100
  270.1 9.5 %copy-start.21 = (s32[8]{0:T(128)S(1)}, s32[8]{0:T(128)}, u32[]{:S(2)}) copy-start(s32[8]{0:T(128)} %get-tuple-element.72) | copy-start | bytes 100
  272.6 59.1 %copy-start.22 = (s32[8]{0:T(128)S(1)}, s32[8]{0:T(128)}, u32[]{:S(2)}) copy-start(s32[8]{0:T(128)} %get-tuple-element.68) | copy-start | bytes 100
  272.6 52.6 %all-to-all-start.4 = ((bf16[16,128,512]{2,1,0:T(8,128)(2,1)}), bf16[16,128,512]{2,1,0:T(8,128)(2,1)S(1)}, u32[]{:S(2)}, u32[]{:S(2)}) async-start(bf16[16,128,512]{2,1,0:T(8,128)(2,1)} %broadcast_select_fusion), calls=%async_computation.4 | async-start | bytes 4194304 | tf_op jit(solution)/shard_map/all_to_all | solution.py:102
  279.5 67.4 %copy-start.16 = (f32[1,1,512]{2,1,0:T(1,128)S(1)}, f32[1,1,512]{2,1,0:T(1,128)}, u32[]{:S(2)}) copy-start(f32[1,1,512]{2,1,0:T(1,128)} %get-tuple-element.113) | copy-start | bytes 6148
  327.8 17.6 %all-to-all-start.6 = ((bf16[8,128,512]{2,1,0:T(8,128)(2,1)}), bf16[8,128,512]{2,1,0:T(8,128)(2,1)S(1)}, u32[]{:S(2)}, u32[]{:S(2)}) async-start(bf16[8,128,512]{2,1,0:T(8,128)(2,1)} %broadcast_select_fusion.3), calls=%async_computation.6 | async-start | bytes 2097152 | tf_op jit(solution)/shard_map/all_to_all | solution.py:111
  346.3 7.0 %copy-start.10 = (bf16[8,128,512]{2,1,0:T(8,128)(2,1)}, bf16[8,128,512]{2,1,0:T(8,128)(2,1)S(1)}, u32[]{:S(2)}) copy-start(bf16[8,128,512]{2,1,0:T(8,128)(2,1)S(1)} %get-tuple-element.93) | copy-start | bytes 3145732
  353.3 138.7 %copy-start.18 = (f32[1,1,512]{2,1,0:T(1,128)S(1)}, f32[1,1,512]{2,1,0:T(1,128)}, u32[]{:S(2)}) copy-start(f32[1,1,512]{2,1,0:T(1,128)} %get-tuple-element.110) | copy-start | bytes 6148
  359.3 3.2 copy-start.5
  374.7 3.2 copy-start.8
  390.1 3.2 copy-start.9
  405.6 3.2 copy-start.3
  411.0 9.1 %copy-start.12 = (bf16[2,512,512]{2,1,0:T(8,128)(2,1)S(1)}, bf16[2,512,512]{2,1,0:T(8,128)(2,1)}, u32[]{:S(2)}) copy-start(bf16[2,512,512]{2,1,0:T(8,128)(2,1)} %get-tuple-element.199) | copy-start | bytes 3145732 | tf_op jit(solution)/shard_map/while
  420.1 1.0 copy-start.13
  426.9 3.2 copy-start.5
  442.3 3.2 copy-start.8
  457.7 3.2 copy-start.9
  473.1 3.2 copy-start.3
  478.5 9.1 %copy-start.12 = (bf16[2,512,512]{2,1,0:T(8,128)(2,1)S(1)}, bf16[2,512,512]{2,1,0:T(8,128)(2,1)}, u32[]{:S(2)}) copy-start(bf16[2,512,512]{2,1,0:T(8,128)(2,1)} %get-tuple-element.199) | copy-start | bytes 3145732 | tf_op jit(solution)/shard_map/while
  487.7 1.0 copy-start.13
  492.1 23.1 %copy-start.1 = (bf16[8,128,512]{2,1,0:T(8,128)(2,1)S(1)}, bf16[8,128,512]{2,1,0:T(8,128)(2,1)}, u32[]{:S(2)}) copy-start(bf16[8,128,512]{2,1,0:T(8,128)(2,1)} %param.17) | copy-start | bytes 3145732
where the time goes:
time: 525 us; the launch traced here: 515 us
  matrix products  221 us (42%)
  waiting for transfers between devices  117 us (22%)
  local copies, waits for them, and re-layouts  84.8 us (16%)
  other arithmetic  49.5 us (9%)
  starting transfers between devices  35.2 us (7%)
  blocking collectives  6.23 us (1%)
    dot_general x16, matrix products, attend_patch(): jnp.einsum('hqk,khd->qhd', probs, values[:, first:first + block], preferr...  140 us
    all_to_all x2, waiting for transfers between devices, per_device(): lax.all_to_all(outgoing, 'gx', split_axis=0, concat_axis=0, tiled=True)  87 us
    while x48, local copies, waits for them, and re-layouts  55.3 us
    dot_general x2, matrix products, encoder_layer(): jnp.dot(hidden, w_down, preferred_element_type=jnp.float32)  45.3 us
    sub x16, other arithmetic, attend_patch(): weights = jnp.exp(scores - peak)  34.8 us
    all_to_all x2, waiting for transfers between devices, per_device(): lax.all_to_all(outgoing, 'gy', split_axis=0, concat_axis=0, tiled=True)  26.2 us
    dot_general x16, matrix products, attend_patch(): jnp.einsum('qhd,khd->hqk', query[:, first:first + block], keys[:, first:f...  20.6 us
    dynamic_slice x8, local copies, waits for them, and re-layouts, encoder_layer(): lax.map(attend_patch, projected.reshape(-1, PATCH, projected.shape[1]))  17.5 us
  transfers between devices with their start and end apart: 7, of which 7 were waited for; matrix products, arithmetic and copies ran while one was open for 2% of the time, Pallas kernels for 0%

commit v1 on v0

v1 whole, which is shorter than its diff:
```python
import functools
import math

import jax
import jax.numpy as jnp
from jax import lax
from jax.experimental import pallas as pl
from jax.experimental.pallas import tpu as pltpu
from jax.sharding import PartitionSpec as P

HEAD_DIM = 16
PATCH = 512
LAYERS = 2
LANES = 128
CHUNKS = 1
UNROLL = 4
FF_BLOCK = 512
BF16 = jnp.bfloat16
F32 = jnp.float32


def normalize(values, gain):
    center = values - jnp.mean(values, axis=1, keepdims=True)
    spread = jnp.mean(center * center, axis=1, keepdims=True)
    return center * lax.rsqrt(spread + 1e-05) * gain


def matmul(left, right, dims=((1,), (0,))):
    return lax.dot_general(left, right, (dims, ((), ())), preferred_element_type=F32)


def layer_kernel(layer, n_in, n_out, order_ref, slot_ref, *refs):
    inputs, refs = refs[:n_in], refs[n_in:]
    gain_ref, *hbm_weights = refs[:5]
    outputs, refs = refs[5 : 5 + n_out], refs[5 + n_out :]
    x_ref, y_ref, q_ref, k_ref, vt_ref, ot_ref, *rest = refs
    weights, (in_sems, out_sems, w_sems) = rest[:4], rest[4:]
    wqkv_ref, wout_ref, wup_ref, wdown_ref = weights
    count, rows, width = x_ref.shape
    heads = width // HEAD_DIM
    per_patch = PATCH // rows
    patch = pl.program_id(0)

    def load(brick, piece):
        span = width // n_in
        return pltpu.make_async_copy(
            inputs[piece].at[order_ref[brick]],
            x_ref.at[brick, :, pl.ds(piece * span, span)],
            in_sems.at[brick, piece],
        )

    def store(brick, piece):
        span = width // n_out
        return pltpu.make_async_copy(
            y_ref.at[brick, :, pl.ds(piece * span, span)],
            outputs[piece].at[slot_ref[brick]],
            out_sems.at[brick, piece],
        )

    def fetch(which):
        return pltpu.make_async_copy(
            hbm_weights[which].at[layer], weights[which], w_sems.at[which]
        )

    def arrive(which):
        @pl.when(patch == 0)
        def _():
            fetch(which).wait()

    @pl.when(patch == 0)
    def _():
        for brick in range(count):
            for piece in range(n_in):
                load(brick, piece).start()
            if brick + 1 == per_patch:
                for which in range(4):
                    fetch(which).start()
        vt_ref[:, HEAD_DIM:, :] = jnp.ones((heads, HEAD_DIM, PATCH), BF16)

    first = patch * per_patch
    for brick in range(per_patch):
        for piece in range(n_in):
            load(first + brick, piece).wait()

    x = x_ref[pl.ds(first, per_patch)].reshape(PATCH, width)
    normed = normalize(x.astype(F32), gain_ref[layer, 0:1, :]).astype(BF16)
    arrive(0)
    scale = math.log2(math.e) / math.sqrt(HEAD_DIM)
    q_ref[...] = (matmul(normed, wqkv_ref[:, :width]) * scale).astype(BF16)
    k_ref[...] = matmul(normed, wqkv_ref[:, width : 2 * width]).astype(BF16)
    values = matmul(normed, wqkv_ref[:, 2 * width :]).T.astype(BF16)
    vt_ref[:, :HEAD_DIM, :] = values.reshape(heads, HEAD_DIM, PATCH)

    lane_head = lax.broadcasted_iota(jnp.int32, (PATCH, LANES), 1) // HEAD_DIM
    per_tile = LANES // HEAD_DIM

    @pl.loop(0, heads // UNROLL)
    def _(group):
        for step in range(UNROLL):
            head = group * UNROLL + step
            column = pl.multiple_of(head // per_tile * LANES, LANES)
            queries = q_ref[:, pl.ds(column, LANES)]
            queries = jnp.where(lane_head == head % per_tile, queries, jnp.zeros_like(queries))
            scores = matmul(k_ref[:, pl.ds(column, LANES)], queries, ((1,), (1,)))
            scores = scores - jnp.max(scores, axis=0, keepdims=True)
            probs = jnp.exp2(scores).astype(BF16)
            mixed = matmul(vt_ref[head], probs)
            spot = pl.ds(pl.multiple_of(head * HEAD_DIM, HEAD_DIM), HEAD_DIM)
            share = 1.0 / mixed[HEAD_DIM : HEAD_DIM + 1]
            ot_ref[spot, :] = (mixed[:HEAD_DIM] * share).astype(BF16)

    arrive(1)
    mixed = (x.astype(F32) + matmul(ot_ref[...], wout_ref[...], ((0,), (0,)))).astype(BF16)
    inner = normalize(mixed.astype(F32), gain_ref[layer, 1:2, :]).astype(BF16)
    total = mixed.astype(F32)
    arrive(2)
    arrive(3)
    for start in range(0, wup_ref.shape[1], FF_BLOCK):
        up = matmul(inner, wup_ref[:, start : start + FF_BLOCK])
        half = up * 0.5
        hidden = (half + half * lax.erf(up * math.sqrt(0.5))).astype(BF16)
        total = total + matmul(hidden, wdown_ref[start : start + FF_BLOCK, :])
    y_ref[pl.ds(first, per_patch)] = total.astype(BF16).reshape(per_patch, rows, width)

    for brick in range(per_patch):
        for piece in range(n_out):
            store(first + brick, piece).start()

    @pl.when(patch == pl.num_programs(0) - 1)
    def _():
        for brick in range(count):
            for piece in range(n_out):
                store(brick, piece).wait()


def encoder_layer(layer, pieces, order, slots, n_slots, n_out, gains, weights):
    n_in = len(pieces)
    rows, width = pieces[0].shape[1], pieces[0].shape[2] * n_in
    count = order.shape[0]
    heads = width // HEAD_DIM
    hbm = pl.BlockSpec(memory_space=pl.ANY)
    smem = pl.BlockSpec(memory_space=pltpu.SMEM)
    vmem = pl.BlockSpec(memory_space=pltpu.VMEM)
    return pl.pallas_call(
        functools.partial(layer_kernel, layer, n_in, n_out),
        grid=(count * rows // PATCH,),
        in_specs=[smem, smem] + [hbm] * n_in + [vmem] + [hbm] * 4,
        out_specs=[hbm] * n_out,
        out_shape=[jax.ShapeDtypeStruct((n_slots, rows, width // n_out), BF16)] * n_out,
        scratch_shapes=[
            pltpu.VMEM((count, rows, width), BF16),
            pltpu.VMEM((count, rows, width), BF16),
            pltpu.VMEM((PATCH, width), BF16),
            pltpu.VMEM((PATCH, width), BF16),
            pltpu.VMEM((heads, 2 * HEAD_DIM, PATCH), BF16),
            pltpu.VMEM((width, PATCH), BF16),
        ]
        + [pltpu.VMEM(weight.shape[1:], BF16) for weight in weights]
        + [
            pltpu.SemaphoreType.DMA((count, n_in)),
            pltpu.SemaphoreType.DMA((count, n_out)),
            pltpu.SemaphoreType.DMA((4,)),
        ],
        compiler_params=pltpu.CompilerParams(vmem_limit_bytes=48 * 2**20),
    )(order, slots, *pieces, gains, *weights)


def ranks(targets):
    count = targets.shape[-1]
    same = targets[..., :, None] == targets[..., None, :]
    earlier = jnp.arange(count)[None, :] < jnp.arange(count)[:, None]
    return jnp.sum((same & earlier).astype(jnp.int32), axis=-1)


def lookup(keys, wanted, found):
    hit = keys[..., None, :] == wanted[..., :, None]
    return jnp.sum(jnp.where(hit, found[..., None, :], 0), axis=-1)


def per_device(points, moved_to, gains, *weights):
    count = points.shape[0]
    peers = {"gx": lax.axis_size("gx"), "gy": lax.axis_size("gy")}
    columns = peers["gy"]
    me = lax.axis_index("gx") * columns + lax.axis_index("gy")
    room = [max(2, -(-count // peers["gx"])), max(2, -(-count // peers["gy"]))]

    def target(moved):
        owner = moved // count
        return jnp.stack([owner[:, 0] // columns, owner[:, 1] % columns], axis=1)

    size = jnp.array(room)[None, :, None]
    local_target = target(moved_to)
    local_slot = local_target * size + ranks(local_target)
    width = points.shape[2] // CHUNKS

    swap = functools.partial(lax.all_to_all, split_axis=0, concat_axis=0, tiled=True)
    devices = peers["gx"] * peers["gy"]
    total = devices * count
    everyone = swap(jnp.broadcast_to(moved_to[None], (devices,) + moved_to.shape), ("gx", "gy"))
    everyone = everyone.transpose(1, 2, 0, 3).reshape(LAYERS, 2, total)
    owners = everyone.reshape(LAYERS, 2, total // count, count)
    whole_target = target(everyone)
    rank = ranks(whole_target.reshape(owners.shape)).reshape(everyone.shape)
    source = jnp.arange(total) // count
    source = jnp.stack([source // columns, source % columns])[None]
    landing = source * size + rank
    mine = me * count + jnp.arange(count)
    mine = jnp.broadcast_to(mine, (LAYERS, 2, count))
    arrival = lookup(everyone, mine, landing)
    second = jnp.arange(peers["gy"] * room[1])
    resend = lookup(
        local_slot[:, 1], jnp.broadcast_to(second, (LAYERS,) + second.shape), arrival[:, 0]
    )

    slots = jnp.arange(peers["gx"] * room[0])
    source = lookup(local_slot[0, 0], slots, jnp.arange(count))
    pieces = [
        jnp.take(points[:, :, i * width : (i + 1) * width], source, axis=0) for i in range(CHUNKS)
    ]
    for layer in range(LAYERS):
        pieces = [swap(piece, "gx") for piece in pieces]
        pieces = [jnp.take(piece, resend[layer], axis=0) for piece in pieces]
        pieces = [swap(piece, "gy") for piece in pieces]
        last = layer + 1 == LAYERS
        pieces = encoder_layer(
            layer,
            pieces,
            arrival[layer, 1],
            jnp.arange(count) if last else local_slot[layer + 1, 0],
            count if last else slots.shape[0],
            1 if last else CHUNKS,
            gains,
            weights,
        )
    return pieces[0]


def solution(mesh):
    placed = (P(("gx", "gy"), None, None), P(None, None, ("gx", "gy")), P(), P(), P(), P(), P())
    return jax.shard_map(
        per_device,
        mesh=mesh,
        in_specs=placed,
        out_specs=P(("gx", "gy"), None, None),
        check_vma=False,
    )
```

time: 525 us -> 256 us (0.49)
  the two profiles are of different devices: /device:TPU:13 before, /device:TPU:0 now
where the time goes in v1:
time: 256 us; the launch traced here: 255 us
  waiting for transfers between devices  114 us (45%)
  Pallas kernels  92.6 us (36%)
  starting transfers between devices  18.8 us (7%)
  blocking collectives  17 us (7%)
  local copies, waits for them, and re-layouts  6.8 us (3%)
  other arithmetic  5.88 us (2%)
    all_to_all x2, waiting for transfers between devices, per_device(): pieces = [swap(piece, 'gx') for piece in pieces]  95.4 us
    pallas_call x2, Pallas kernels, encoder_layer(): pl.pallas_call(functools.partial(layer_kernel, layer, n_in, n_out), grid=...  92.6 us
    all_to_all x1, blocking collectives, per_device(): pieces = [swap(piece, 'gy') for piece in pieces]  17 us
    all_to_all x1, waiting for transfers between devices, per_device(): pieces = [swap(piece, 'gy') for piece in pieces]  14.4 us
    all_to_all x2, starting transfers between devices, per_device(): pieces = [swap(piece, 'gx') for piece in pieces]  7.95 us
    all_to_all x1, starting transfers between devices, per_device(): swap(jnp.broadcast_to(moved_to[None], (devices,) + moved_to.shape), ('gx'...  7.3 us
  transfers between devices with their start and end apart: 4, of which 4 were waited for; matrix products, arithmetic and copies ran while one was open for 2% of the time, Pallas kernels for 0%

profile of v1, /device:TPU:0, one launch (start us, length us, event | category | flops | bytes accessed | tf_op | source)
XLA Modules:
  0.0 255.3 jit_solution(14805889091132013887)
XLA Ops:
  0.0 0.0 copy-start
  0.0 1.4 broadcast_in_dim.76
  1.4 7.3 %all-to-all-start = ((s32[32,2,2,8]{3,2,1,0:T(2,128)}), s32[32,2,2,8]{3,2,1,0:T(2,128)S(1)}, u32[]{:S(2)}, u32[]{:S(2)}) async-start(s32[32,2,2,8]{3,2,1,0:T(2,128)} %broadcast_in_dim.76), calls=%async_computation | async-start | bytes 131072 | tf_op jit(solution)/shard_map/all_to_all | solution.py:199
  8.7 0.7 and_select_fusion.5
  9.5 0.2 convert_reduce_fusion.1
  9.7 0.1 select_reduce_fusion.2
  9.8 0.0 copy-done
  9.8 0.7 gather_fusion
  10.5 1.6 broadcast_select_fusion
  12.1 4.0 %all-to-all-done = s32[32,2,2,8]{3,2,1,0:T(2,128)S(1)} async-done(((s32[32,2,2,8]{3,2,1,0:T(2,128)}), s32[32,2,2,8]{3,2,1,0:T(2,128)S(1)}, u32[]{:S(2)}, u32[]{:S(2)}) %all-to-all-start) | async-done | bytes 4128 | tf_op jit(solution)/shard_map/all_to_all | solution.py:199
  16.1 3.6 %all-to-all-start.1 = ((bf16[16,128,512]{2,1,0:T(8,128)(2,1)}), bf16[16,128,512]{2,1,0:T(8,128)(2,1)S(1)}, u32[]{:S(2)}, u32[]{:S(2)}) async-start(bf16[16,128,512]{2,1,0:T(8,128)(2,1)} %broadcast_select_fusion), calls=%async_computation.1 | async-start | bytes 4194304 | tf_op jit(solution)/shard_map/all_to_all | solution.py:221
  19.8 0.1 eq.71
  20.0 0.1 stack.30
  20.1 0.1 stack.27
  20.2 0.1 stack.29
  20.3 0.1 stack.26
  20.4 0.1 copy.24
  20.4 0.1 copy.23
  20.5 0.1 copy.22
  20.6 0.1 copy.21
  20.6 0.1 convert_reduce_fusion
  20.8 0.1 copy.25
  20.8 0.1 reshape.192
  21.0 0.2 select_reduce_fusion
  21.2 0.1 select_reduce_fusion.1
  21.4 47.1 %all-to-all-done.1 = bf16[16,128,512]{2,1,0:T(8,128)(2,1)S(1)} async-done(((bf16[16,128,512]{2,1,0:T(8,128)(2,1)}), bf16[16,128,512]{2,1,0:T(8,128)(2,1)S(1)}, u32[]{:S(2)}, u32[]{:S(2)}) %all-to-all-start.1) | async-done | bytes 2097184 | tf_op jit(solution)/shard_map/all_to_all | solution.py:221
  68.5 1.6 gather_fusion.1
  70.0 0.0 copy-start.2
  70.0 0.0 copy-start.3
  70.0 2.4 broadcast_select_fusion.2
  72.5 3.5 %all-to-all-start.2 = ((bf16[8,128,512]{2,1,0:T(8,128)(2,1)}), bf16[8,128,512]{2,1,0:T(8,128)(2,1)S(1)}, u32[]{:S(2)}, u32[]{:S(2)}) async-start(bf16[8,128,512]{2,1,0:T(8,128)(2,1)} %broadcast_select_fusion.2), calls=%async_computation.2 | async-start | bytes 2097152 | tf_op jit(solution)/shard_map/all_to_all | solution.py:223
  76.0 14.4 %all-to-all-done.2.refs_0_ = bf16[8,128,512]{2,1,0:T(8,128)(2,1)S(1)} async-done(((bf16[8,128,512]{2,1,0:T(8,128)(2,1)}), bf16[8,128,512]{2,1,0:T(8,128)(2,1)S(1)}, u32[]{:S(2)}, u32[]{:S(2)}) %all-to-all-start.2) | async-done | bytes 1048608 | tf_op jit(solution)/shard_map/all_to_all | solution.py:223
  90.4 0.0 copy-done.2
  90.4 0.0 copy-done.3
  90.5 46.4 %shard_map.82 = bf16[16,128,512]{2,1,0:T(8,128)(2,1)} custom-call(s32[8]{0:T(128)S(1)} %get-tuple-element.16.order_ref, s32[8]{0:T(128)S(1)} %get-tuple-element.13.slot_ref, bf16[8,128,512]{2,1,0:T(8,128)(2,1)S(1)} %all-to-all-done.2.refs_0_, f32[2,2,512]{2,1,0:T(2,128)S(1)} %copy-done.3, bf16[2,512,1536]{2,1,0:T(8,128)(2,1)} %refs_2_.3, ...), custom_call_target="tpu_custom_call" | custom-call | tf_op jit(solution)/shard_map/pallas_call | solution.py:144
  136.9 4.4 %all-to-all-start.3 = ((bf16[16,128,512]{2,1,0:T(8,128)(2,1)}), bf16[16,128,512]{2,1,0:T(8,128)(2,1)}, u32[]{:S(2)}, u32[]{:S(2)}) async-start(bf16[16,128,512]{2,1,0:T(8,128)(2,1)} %shard_map.82), calls=%async_computation.3 | async-start | bytes 4194304 | tf_op jit(solution)/shard_map/all_to_all | solution.py:221
  141.3 48.3 %all-to-all-done.3 = bf16[16,128,512]{2,1,0:T(8,128)(2,1)} async-done(((bf16[16,128,512]{2,1,0:T(8,128)(2,1)}), bf16[16,128,512]{2,1,0:T(8,128)(2,1)}, u32[]{:S(2)}, u32[]{:S(2)}) %all-to-all-start.3) | async-done | bytes 2097184 | tf_op jit(solution)/shard_map/all_to_all | solution.py:221
  189.6 2.2 gather_fusion.2
  191.8 0.0 copy-start.1
  191.8 0.2 broadcast_select_fusion.1
  192.0 17.0 %all_to_all.25.refs_0_ = bf16[8,128,512]{2,1,0:T(8,128)(2,1)S(1)} all-to-all(bf16[8,128,512]{2,1,0:T(8,128)(2,1)S(1)} %broadcast_select_fusion.1), channel_id=1, replica_groups=mesh['gx'=8,'gy'=4] {'gy'}, dimensions={0} | all-to-all | bytes 2097152 | tf_op jit(solution)/shard_map/all_to_all | solution.py:223
  209.0 0.0 copy-done.1
  209.0 46.2 %shard_map.83 = bf16[8,128,512]{2,1,0:T(8,128)(2,1)} custom-call(s32[8]{0:T(128)S(1)} %get-tuple-element.17.order_ref, s32[8]{0:T(128)S(1)} %iota.49.slot_ref, bf16[8,128,512]{2,1,0:T(8,128)(2,1)S(1)} %all_to_all.25.refs_0_, f32[2,2,512]{2,1,0:T(2,128)S(1)} %copy-done.3, bf16[2,512,1536]{2,1,0:T(8,128)(2,1)S(1)} %copy-done.1, ...), custom_call_target="tpu_custom_call" | custom-call | tf_op jit(solution)/shard_map/pallas_call | solution.py:144
  (24 shorter events, 0.2 us)
Async XLA Ops:
  0.0 9.8 %copy-start = (bf16[8,128,512]{2,1,0:T(8,128)(2,1)S(1)}, bf16[8,128,512]{2,1,0:T(8,128)(2,1)}, u32[]{:S(2)}) copy-start(bf16[8,128,512]{2,1,0:T(8,128)(2,1)} %param.10) | copy-start | bytes 3145732
  1.4 14.7 %all-to-all-start = ((s32[32,2,2,8]{3,2,1,0:T(2,128)}), s32[32,2,2,8]{3,2,1,0:T(2,128)S(1)}, u32[]{:S(2)}, u32[]{:S(2)}) async-start(s32[32,2,2,8]{3,2,1,0:T(2,128)} %broadcast_in_dim.76), calls=%async_computation | async-start | bytes 131072 | tf_op jit(solution)/shard_map/all_to_all | solution.py:199
  16.1 52.3 %all-to-all-start.1 = ((bf16[16,128,512]{2,1,0:T(8,128)(2,1)}), bf16[16,128,512]{2,1,0:T(8,128)(2,1)S(1)}, u32[]{:S(2)}, u32[]{:S(2)}) async-start(bf16[16,128,512]{2,1,0:T(8,128)(2,1)} %broadcast_select_fusion), calls=%async_computation.1 | async-start | bytes 4194304 | tf_op jit(solution)/shard_map/all_to_all | solution.py:221
  70.0 20.4 %copy-start.2 = (bf16[2,512,512]{2,1,0:T(8,128)(2,1)S(1)}, bf16[2,512,512]{2,1,0:T(8,128)(2,1)}, u32[]{:S(2)}) copy-start(bf16[2,512,512]{2,1,0:T(8,128)(2,1)} %refs_3_.3) | copy-start | bytes 3145732
  70.0 20.4 %copy-start.3 = (f32[2,2,512]{2,1,0:T(2,128)S(1)}, f32[2,2,512]{2,1,0:T(2,128)}, u32[]{:S(2)}) copy-start(f32[2,2,512]{2,1,0:T(2,128)} %refs_1_.3) | copy-start | bytes 24580
  72.5 18.0 %all-to-all-start.2 = ((bf16[8,128,512]{2,1,0:T(8,128)(2,1)}), bf16[8,128,512]{2,1,0:T(8,128)(2,1)S(1)}, u32[]{:S(2)}, u32[]{:S(2)}) async-start(bf16[8,128,512]{2,1,0:T(8,128)(2,1)} %broadcast_select_fusion.2), calls=%async_computation.2 | async-start | bytes 2097152 | tf_op jit(solution)/shard_map/all_to_all | solution.py:223
  136.9 52.7 %all-to-all-start.3 = ((bf16[16,128,512]{2,1,0:T(8,128)(2,1)}), bf16[16,128,512]{2,1,0:T(8,128)(2,1)}, u32[]{:S(2)}, u32[]{:S(2)}) async-start(bf16[16,128,512]{2,1,0:T(8,128)(2,1)} %shard_map.82), calls=%async_computation.3 | async-start | bytes 4194304 | tf_op jit(solution)/shard_map/all_to_all | solution.py:221
  191.8 17.2 %copy-start.1 = (bf16[2,512,1536]{2,1,0:T(8,128)(2,1)S(1)}, bf16[2,512,1536]{2,1,0:T(8,128)(2,1)}, u32[]{:S(2)}) copy-start(bf16[2,512,1536]{2,1,0:T(8,128)(2,1)} %refs_2_.3) | copy-start | bytes 9437188

commit v2 on v1

v2 whole, which is shorter than its diff:
```python
import functools
import math

import jax
import jax.numpy as jnp
from jax import lax
from jax.experimental import pallas as pl
from jax.experimental.pallas import tpu as pltpu
from jax.sharding import PartitionSpec as P

HEAD_DIM = 16
PATCH = 512
LAYERS = 2
LANES = 128
WAYS = 4
FF_BLOCK = 512
BF16 = jnp.bfloat16
F32 = jnp.float32
HBM = pl.BlockSpec(memory_space=pltpu.HBM)
SMEM = pl.BlockSpec(memory_space=pltpu.SMEM)
VMEM = pl.BlockSpec(memory_space=pltpu.VMEM)


def normalize(values, gain):
    center = values - jnp.mean(values, axis=1, keepdims=True)
    spread = jnp.mean(center * center, axis=1, keepdims=True)
    return center * lax.rsqrt(spread + 1e-05) * gain


def matmul(left, right, dims=((1,), (0,))):
    return lax.dot_general(left, right, (dims, ((), ())), preferred_element_type=F32)


def start(copy):
    copy.start()


def wait(copy):
    copy.wait()


def send_bricks(action, patch, bricks, tables, payload, spare, hops, sems):
    pick_ref, spare_ref = tables
    size, rows, width = bricks.shape
    peers = len(payload)

    def here(brick):
        return (brick >= patch * size) & (brick < (patch + 1) * size)

    for shift in range(peers):
        brick = pick_ref[shift]

        @pl.when(here(brick))
        def _():
            source = bricks.at[brick - patch * size]
            action(
                pltpu.make_async_copy(source, payload[shift].at[pl.ds(0, rows)], sems.at[0, shift])
            )

    for place in range(spare.shape[0]):
        brick = spare_ref[place]

        @pl.when(here(brick))
        def _():
            source = bricks.at[brick - patch * size]
            action(pltpu.make_async_copy(source, spare.at[place], sems.at[1, place]))

    brick = spare_ref[0]

    @pl.when(here(brick))
    def _():
        source = bricks.at[brick - patch * size]
        tall = rows // len(hops)
        for way in range(len(hops)):
            window = pl.ds(way * tall, tall)
            action(pltpu.make_async_copy(source.at[window], hops[way], sems.at[2, way]))


def pack_kernel(pick_ref, spare_ref, points, *refs):
    peers = pick_ref.shape[0]
    payload, spare, hops, sems = refs[:peers], refs[peers], refs[peers + 1 : -1], refs[-1]
    for action in (start, wait):
        send_bricks(action, 0, points, (pick_ref, spare_ref), payload, spare, hops, sems)


def relay_kernel(ways, relay_ref, *refs):
    peers = relay_ref.shape[0]
    hops, payload = refs[:ways], refs[ways + peers : ways + 2 * peers]
    staged, in_sems, out_sems = refs[ways + 2 * peers :]
    _, tall, _ = staged.shape
    rows = payload[0].shape[0] - tall
    for action in (start, wait):
        for way in range(ways):
            action(pltpu.make_async_copy(hops[way], staged.at[way], in_sems.at[way]))
    for action in (start, wait):
        for shift in range(peers):

            @pl.when(relay_ref[shift] >= 0)
            def _():
                action(
                    pltpu.make_async_copy(
                        staged.at[relay_ref[shift]],
                        payload[shift].at[pl.ds(rows, tall)],
                        out_sems.at[shift],
                    )
                )


def turn_kernel(peers, kind_ref, source_ref, *refs):
    arrived, second, refs = refs[:peers], refs[peers], refs[peers + 1 :]
    outs, (staged, extra, in_sems, out_sems) = refs[:-4], refs[-4:]
    room, rows, width = outs[0].shape
    tall = rows // WAYS
    stride = peers // WAYS
    for action in (start, wait):
        for shift in range(peers):
            action(pltpu.make_async_copy(arrived[shift], staged.at[shift], in_sems.at[shift]))
    for slot in range(kind_ref.shape[0]):
        out, sem = outs[slot // room].at[slot % room], out_sems.at[slot]

        @pl.when(kind_ref[slot] == 0)
        def _():
            pltpu.make_async_copy(
                staged.at[source_ref[slot], pl.ds(0, rows)], out, sem
            ).start()

        @pl.when(kind_ref[slot] == 1)
        def _():
            for way in range(WAYS):
                shift = (source_ref[slot] - way * stride + peers) % peers
                pltpu.make_async_copy(
                    staged.at[shift, pl.ds(rows, tall)], out.at[pl.ds(way * tall, tall)], sem
                ).start()

        @pl.when(kind_ref[slot] == 2)
        def _():
            copy = pltpu.make_async_copy(
                second.at[source_ref[slot]], extra.at[slot], in_sems.at[peers + slot]
            )
            copy.start()
            copy.wait()
            pltpu.make_async_copy(extra.at[slot], out, sem).start()

    for slot in range(kind_ref.shape[0]):
        out = outs[slot // room].at[slot % room]
        pltpu.make_async_copy(extra.at[slot], out, out_sems.at[slot]).wait()


def attend(q_ref, k_ref, v_ref, mixed_ref):
    tiles, count, _ = v_ref.shape
    head_of = lax.broadcasted_iota(jnp.int32, (count, LANES), 1) // HEAD_DIM
    per_tile = LANES // HEAD_DIM

    def weigh(queries, keys, values, head, shifted):
        chosen = jnp.where(head_of == head, queries, jnp.zeros_like(queries))
        scores = matmul(chosen, keys, ((1,), (1,)))
        if shifted:
            scores = scores - jnp.max(scores, axis=1, keepdims=True)
        return matmul(jnp.exp2(scores).astype(BF16), values)

    low = jnp.full((count, LANES), 1.0, F32)
    high = jnp.full((count, LANES), 1.0, F32)
    for tile in range(tiles):
        column = pl.ds(tile * LANES, LANES)
        queries, keys, values = q_ref[:, column], k_ref[:, column], v_ref[tile]
        above = jnp.zeros((count, LANES), F32)
        below = jnp.ones((count, LANES), F32)
        for head in range(per_tile):
            sums = weigh(queries, keys, values, head, False)
            above = jnp.where(head_of == head, sums[:, :LANES], above)
            below = jnp.where(head_of == head, sums[:, LANES:], below)
        mixed_ref[:, column] = (above / below).astype(BF16)
        low = jnp.minimum(low, below)
        high = jnp.maximum(high, below)
    safe = (jnp.min(low) > 2.0**-60) & (jnp.max(high) < 2.0**100)

    @pl.when(jnp.logical_not(safe))
    def _():
        @pl.loop(0, tiles)
        def _(tile):
            column = pl.ds(pl.multiple_of(tile * LANES, LANES), LANES)

            @pl.loop(0, per_tile)
            def _(head):
                sums = weigh(q_ref[:, column], k_ref[:, column], v_ref[tile], head, True)
                mixed = (sums[:, :LANES] / sums[:, LANES:]).astype(BF16)
                mixed_ref[:, column] = jnp.where(head_of == head, mixed, mixed_ref[:, column])


def layer_kernel(layer, columns, peers, order_ref, *refs):
    tables, refs = refs[:2], refs[2:]
    arrived, gain_ref = refs[:columns], refs[columns]
    hbm_weights, refs = refs[columns + 1 : columns + 5], refs[columns + 5 :]
    n_out = peers + 1 + WAYS if peers else 1
    outputs, refs = refs[:n_out], refs[n_out:]
    x_ref, y_ref, q_ref, k_ref, v_ref, mixed_ref = refs[:6]
    weights, (in_sems, out_sems, w_sems) = refs[6:10], refs[10:]
    wqkv_ref, wout_ref, wup_ref, wdown_ref = weights
    patches, per_patch, rows, width = y_ref.shape
    room = arrived[0].shape[0]
    turn = pl.program_id(0)

    def load(piece):
        return pltpu.make_async_copy(
            arrived[piece], x_ref.at[pl.ds(piece * room, room)], in_sems.at[piece]
        )

    def store(action, step):
        if peers:
            send_bricks(
                action, step, y_ref.at[step], tables, outputs[:peers], outputs[peers],
                outputs[peers + 1 :], out_sems,
            )
        else:
            spot = pl.ds(step * per_patch, per_patch)
            action(pltpu.make_async_copy(y_ref.at[step], outputs[0].at[spot], out_sems.at[0, step]))

    def fetch(which):
        return pltpu.make_async_copy(
            hbm_weights[which].at[layer], weights[which], w_sems.at[which]
        )

    def arrive(which):
        @pl.when(turn == 0)
        def _():
            fetch(which).wait()

    @pl.when(turn == 0)
    def _():
        for piece in range(columns):
            load(piece).start()
        for which in range(4):
            fetch(which).start()
        v_ref[:, :, LANES:] = jnp.ones(v_ref.shape[:2] + (LANES,), BF16)
        for piece in range(columns):
            load(piece).wait()

    first = turn * per_patch
    x = jnp.concatenate([x_ref[order_ref[first + brick]] for brick in range(per_patch)], axis=0)
    normed = normalize(x.astype(F32), gain_ref[layer, 0:1, :]).astype(BF16)
    arrive(0)
    scale = math.log2(math.e) / math.sqrt(HEAD_DIM)
    q_ref[...] = (matmul(normed, wqkv_ref[:, :width]) * scale).astype(BF16)
    k_ref[...] = matmul(normed, wqkv_ref[:, width : 2 * width]).astype(BF16)
    values = matmul(normed, wqkv_ref[:, 2 * width :]).astype(BF16)
    for tile in range(width // LANES):
        v_ref[tile, :, :LANES] = values[:, tile * LANES : (tile + 1) * LANES]

    attend(q_ref, k_ref, v_ref, mixed_ref)

    arrive(1)
    mixed = (x.astype(F32) + matmul(mixed_ref[...], wout_ref[...])).astype(BF16)
    inner = normalize(mixed.astype(F32), gain_ref[layer, 1:2, :]).astype(BF16)
    total = mixed.astype(F32)
    arrive(2)
    arrive(3)
    for begin in range(0, wup_ref.shape[1], FF_BLOCK):
        up = matmul(inner, wup_ref[:, begin : begin + FF_BLOCK])
        half = up * 0.5
        hidden = (half + half * lax.erf(up * math.sqrt(0.5))).astype(BF16)
        total = total + matmul(hidden, wdown_ref[begin : begin + FF_BLOCK, :])
    y_ref[turn] = total.astype(BF16).reshape(per_patch, rows, width)
    store(start, turn)

    @pl.when(turn == patches - 1)
    def _():
        for step in range(patches):
            store(wait, step)


def send_shapes(count, rows, width, peers):
    tall = rows // WAYS
    shapes = [jax.ShapeDtypeStruct((rows + tall, width), BF16)] * peers
    shapes += [jax.ShapeDtypeStruct((max(1, count // 2), rows, width), BF16)]
    return shapes + [jax.ShapeDtypeStruct((tall, width), BF16)] * WAYS


def pack(points, tables):
    count, rows, width = points.shape
    peers = tables[0].shape[0]
    shapes = send_shapes(count, rows, width, peers)
    return pl.pallas_call(
        pack_kernel,
        in_specs=[SMEM] * 2 + [VMEM],
        out_specs=[HBM] * len(shapes),
        out_shape=shapes,
        scratch_shapes=[pltpu.SemaphoreType.DMA((3, max(peers, count)))],
    )(*tables, points)


def relay(picks, hops, payload):
    peers = len(payload)
    return pl.pallas_call(
        functools.partial(relay_kernel, len(hops)),
        in_specs=[SMEM] + [HBM] * (len(hops) + peers),
        out_specs=[HBM] * peers,
        out_shape=[jax.ShapeDtypeStruct(slot.shape, BF16) for slot in payload],
        input_output_aliases={1 + len(hops) + i: i for i in range(peers)},
        scratch_shapes=[
            pltpu.VMEM((len(hops),) + hops[0].shape, BF16),
            pltpu.SemaphoreType.DMA((len(hops),)),
            pltpu.SemaphoreType.DMA((peers,)),
        ],
    )(picks, *hops, *payload)


def turn_bricks(kind, source, arrived, second, columns):
    peers, slots = len(arrived), kind.shape[0]
    brick = second.shape[1:]
    return pl.pallas_call(
        functools.partial(turn_kernel, peers),
        in_specs=[SMEM] * 2 + [HBM] * (peers + 1),
        out_specs=[HBM] * columns,
        out_shape=[jax.ShapeDtypeStruct((slots // columns,) + brick, BF16)] * columns,
        scratch_shapes=[
            pltpu.VMEM((peers,) + arrived[0].shape, BF16),
            pltpu.VMEM((slots,) + brick, BF16),
            pltpu.SemaphoreType.DMA((peers + slots,)),
            pltpu.SemaphoreType.DMA((slots,)),
        ],
        compiler_params=pltpu.CompilerParams(vmem_limit_bytes=32 * 2**20),
    )(kind, source, *arrived, second)


def encoder_layer(layer, arrived, order, tables, gains, weights, last=False):
    columns = len(arrived)
    room, rows, width = arrived[0].shape
    count = order.shape[0]
    patches = count * rows // PATCH
    per_patch = PATCH // rows
    peers = 0 if last else tables[0].shape[0]
    if last:
        shapes = [jax.ShapeDtypeStruct((count, rows, width), BF16)]
    else:
        shapes = send_shapes(count, rows, width, peers)
    tokens = patches * PATCH
    dense = sum(2 * tokens * weight.shape[1] * weight.shape[2] for weight in weights)
    heads = width // HEAD_DIM
    return pl.pallas_call(
        functools.partial(layer_kernel, layer, columns, peers),
        grid=(patches,),
        in_specs=[SMEM] * 3 + [HBM] * columns + [VMEM] + [HBM] * 4,
        out_specs=[HBM] * len(shapes),
        out_shape=shapes,
        scratch_shapes=[
            pltpu.VMEM((columns * room, rows, width), BF16),
            pltpu.VMEM((patches, per_patch, rows, width), BF16),
            pltpu.VMEM((PATCH, width), BF16),
            pltpu.VMEM((PATCH, width), BF16),
            pltpu.VMEM((width // LANES, PATCH, 2 * LANES), BF16),
            pltpu.VMEM((PATCH, width), BF16),
        ]
        + [pltpu.VMEM(weight.shape[1:], BF16) for weight in weights]
        + [
            pltpu.SemaphoreType.DMA((columns,)),
            pltpu.SemaphoreType.DMA((3, max(count, peers))),
            pltpu.SemaphoreType.DMA((4,)),
        ],
        compiler_params=pltpu.CompilerParams(vmem_limit_bytes=48 * 2**20),
        cost_estimate=pl.CostEstimate(
            flops=dense + 8 * tokens * PATCH * heads * LANES,
            bytes_accessed=4 * tokens * width + sum(2 * w.shape[1] * w.shape[2] for w in weights),
            transcendentals=tokens * PATCH * heads,
        ),
    )(order, *tables, *arrived, gains, *weights)


def ranks(targets):
    count = targets.shape[-1]
    same = targets[..., :, None] == targets[..., None, :]
    earlier = jnp.arange(count)[None, :] < jnp.arange(count)[:, None]
    return jnp.sum((same & earlier).astype(jnp.int32), axis=-1)


def lookup(keys, wanted, found):
    hit = keys[..., None, :] == wanted[..., :, None]
    return jnp.sum(jnp.where(hit, found[..., None, :], 0), axis=-1)


def most(keys, values, chosen):
    hit = (keys[..., None, :] == values[:, None]) & chosen[..., None, :]
    return jnp.max(jnp.sum(hit.astype(jnp.int32), axis=-1))


def shifted(arrays, axis):
    size = lax.axis_size(axis)
    step = size // len(arrays)
    return [arrays[0]] + [
        lax.ppermute(arrays[d], axis, [(i, (i + d * step) % size) for i in range(size)])
        for d in range(1, len(arrays))
    ]


def per_device(points, moved_to, gains, *weights):
    count, rows, width = points.shape
    peers, columns = lax.axis_size("gx"), lax.axis_size("gy")
    row, column = lax.axis_index("gx"), lax.axis_index("gy")
    me = row * columns + column
    devices = peers * columns
    total = devices * count
    room = max(2, -(-count // columns))
    swap = functools.partial(lax.all_to_all, split_axis=0, concat_axis=0, tiled=True)
    bricks = jnp.arange(count)
    shifts = jnp.arange(peers)
    stride = peers // WAYS

    ahead = (moved_to[:, 0] // count // columns - row) % peers
    late = ranks(ahead) > 0
    pick = lookup(jnp.where(late, -1, ahead), shifts, bricks + 1) - 1
    place = jnp.where(late, jnp.cumsum(late.astype(jnp.int32), axis=1) - 1, -1)
    spare = lookup(place, jnp.arange(max(1, count // 2)), bricks + 1) - 1
    across = (moved_to[:, 1] // count - column) % columns
    across_slot = across * room + ranks(across)
    tables = [(pick[layer], spare[layer]) for layer in range(LAYERS)]

    everyone = swap(jnp.broadcast_to(moved_to[None], (devices,) + moved_to.shape), ("gx", "gy"))
    targets = everyone[:, :, 0] // count // columns
    behind = ranks(targets) > 0
    opening = behind & (jnp.cumsum(behind.astype(jnp.int32), axis=-1) == 1)
    relayed = jnp.sum(jnp.where(opening, targets + 1, 0), axis=-1) - 1
    flat = lambda values: values.transpose(1, 0, 2).reshape(LAYERS, total)
    first, second = flat(everyone[:, :, 0]), flat(everyone[:, :, 1])
    behind = flat(behind)
    owner = jnp.arange(total) // count

    def crowded(layer):
        out = jnp.sum(behind[layer].reshape(devices, count).astype(jnp.int32), axis=1)
        return (jnp.max(out) > 1) | (
            most(first[layer] // count, jnp.arange(devices), behind[layer]) > 1
        )

    across_rank = flat(ranks(everyone[:, :, 1] // count % columns))
    mine = me * count + bricks
    slots = jnp.arange(columns * room)
    every = jnp.arange(devices)
    in_column = every % columns == column
    plans = []
    for layer in range(LAYERS):
        extra = crowded(layer)
        goal = jnp.where(in_column & (relayed[:, layer] >= 0), (relayed[:, layer] - row) % peers, -1)
        behind_me = (row - every // columns) % peers
        hit = (goal[None, :] == shifts[:, None]) & (behind_me % stride == 0)[None, :]
        relays = jnp.max(jnp.where(hit, behind_me[None, :] // stride, -1), axis=1)
        origin = lookup(first[layer], mine, (row - owner // columns) % peers)
        kind = lookup(first[layer], mine, jnp.where(behind[layer], jnp.where(extra, 2, 1), 0))
        slot_kind = lookup(across_slot[layer], slots, kind)
        slot_origin = lookup(across_slot[layer], slots, origin)
        order = lookup(
            second[layer], mine, (column - owner % columns) % columns * room + across_rank[layer]
        )
        plans.append((extra, relays, slot_kind, slot_origin, order))

    made = pack(points, tables[0])
    for layer in range(LAYERS):
        extra, relays, slot_kind, slot_origin, order = plans[layer]
        payload, spares, hops = made[:peers], made[peers], made[peers + 1 :]
        hops = shifted(hops, "gx")
        payload = relay(relays, hops, payload)
        arrived = shifted(payload, "gx")

        def send_second(spares, layer=layer):
            target = (ahead[layer] + row) % peers
            ready = lookup(jnp.where(late[layer], target, -1), shifts, place[layer])
            landed = swap(jnp.take(spares, ready, axis=0), "gx")
            return jnp.take(landed, (row - shifts) % peers, axis=0)

        def send_nothing(spares):
            return jnp.zeros((peers, rows, width), BF16)

        spares, arrived[1] = lax.optimization_barrier((spares, arrived[1]))
        seconds = lax.cond(extra, send_second, send_nothing, spares)
        arrived = turn_bricks(slot_kind, slot_origin, arrived, seconds, columns)
        arrived = shifted(arrived, "gy")
        last = layer + 1 == LAYERS
        made = encoder_layer(
            layer, arrived, order, tables[(layer + 1) % LAYERS], gains, weights, last
        )
    return made[0]


def solution(mesh):
    placed = (P(("gx", "gy"), None, None), P(None, None, ("gx", "gy")), P(), P(), P(), P(), P())
    return jax.shard_map(
        per_device,
        mesh=mesh,
        in_specs=placed,
        out_specs=P(("gx", "gy"), None, None),
        check_vma=False,
    )
```

time: 256 us -> 307 us (1.20)
  the two profiles are of different devices: /device:TPU:0 before, /device:TPU:13 now
where the time goes in v2:
time: 307 us; the launch traced here: 306 us
  Pallas kernels  174 us (57%)
  waiting for transfers between devices  78.7 us (26%)
  starting transfers between devices  29.5 us (10%)
  local copies, waits for them, and re-layouts  15.2 us (5%)
  other arithmetic  5.75 us (2%)
  between operations  3.18 us (1%)
    pallas_call x2, Pallas kernels, encoder_layer(): pl.pallas_call(functools.partial(layer_kernel, layer, columns, peers), gr...  159 us
    ppermute x26, waiting for transfers between devices, shifted(): lax.ppermute(arrays[d], axis, [(i, (i + d * step) % size) for i in range(...  78.7 us
    ppermute x26, starting transfers between devices, shifted(): lax.ppermute(arrays[d], axis, [(i, (i + d * step) % size) for i in range(...  23.2 us
    unnamed x48, local copies, waits for them, and re-layouts  9.94 us
    pallas_call x2, Pallas kernels, turn_bricks(): pl.pallas_call(functools.partial(turn_kernel, peers), in_specs=[SMEM] * 2...  8.1 us
    all_to_all x1, starting transfers between devices, per_device(): swap(jnp.broadcast_to(moved_to[None], (devices,) + moved_to.shape), ('gx'...  6.3 us
  transfers between devices with their start and end apart: 27, of which 20 were waited for; matrix products, arithmetic and copies ran while one was open for 3% of the time, Pallas kernels for 1%

profile of v2, /device:TPU:13, one launch (start us, length us, event | category | flops | bytes accessed | tf_op | source)
XLA Modules:
  0.0 306.4 jit_solution(1609667746906288140)
XLA Ops:
  0.0 0.7 copy.42
  0.7 0.6 broadcast_in_dim.246
  1.3 6.3 %all-to-all-start.2 = ((s32[32,2,2,8]{3,1,2,0:T(2,128)}), s32[32,2,2,8]{3,1,2,0:T(2,128)S(1)}, u32[]{:S(2)}, u32[]{:S(2)}) async-start(s32[32,2,2,8]{3,1,2,0:T(2,128)} %broadcast_in_dim.246), calls=%async_computation.2 | async-start | bytes 131072 | tf_op jit(solution)/shard_map/all_to_all | solution.py:416
  8.1 0.6 slice_bitcast_fusion.4
  9.5 2.4 shard_map.73
  12.0 1.3 collective-permute-start
  13.2 1.2 collective-permute-start.1
  14.4 1.3 collective-permute-start.2
  17.1 0.7 reduce_max.57
  17.9 0.7 reduce_max.58
  20.7 0.7 select_reduce_fusion.6
  21.5 0.7 reduce_max.54
  22.8 0.7 reduce_max.55
  24.5 0.6 copy-done.16
  25.1 2.2 shard_map.74
  27.9 3.9 %collective-permute-start.5 = (bf16[160,512]{1,0:T(8,128)(2,1)}, bf16[160,512]{1,0:T(8,128)(2,1)S(1)}, u32[]{:S(2)}, u32[]{:S(2)}) collective-permute-start(bf16[160,512]{1,0:T(8,128)(2,1)} %get-tuple-element.124), channel_id=1, source_target_pairs={{0,12},{4,16},{8,20},{12,24},{16,28},{20,0},{24,4},{28,8},{1,13},{... | collective-permute-start | bytes 491528 | tf_op jit(solution)/shard_map/ppermute | solution.py:389
  31.8 1.5 collective-permute-start.7
  33.3 2.0 collective-permute-start.8
  35.7 0.5 collective-permute-start.9
  36.6 1.1 conditional.2
  36.7 1.1 broadcast.1035
  37.7 13.5 %collective-permute-done.5.refs_3_ = bf16[160,512]{1,0:T(8,128)(2,1)S(1)} collective-permute-done((bf16[160,512]{1,0:T(8,128)(2,1)}, bf16[160,512]{1,0:T(8,128)(2,1)S(1)}, u32[]{:S(2)}, u32[]{:S(2)}) %collective-permute-start.5) | collective-permute-done | bytes 163872 | tf_op jit(solution)/shard_map/ppermute | solution.py:389
  51.2 3.7 %collective-permute-done.6.refs_4_ = bf16[160,512]{1,0:T(8,128)(2,1)S(1)} collective-permute-done((bf16[160,512]{1,0:T(8,128)(2,1)}, bf16[160,512]{1,0:T(8,128)(2,1)S(1)}, u32[]{:S(2)}, u32[]{:S(2)}) %collective-permute-start.6) | collective-permute-done | bytes 163872 | tf_op jit(solution)/shard_map/ppermute | solution.py:389
  54.9 5.2 %collective-permute-done.8.refs_6_ = bf16[160,512]{1,0:T(8,128)(2,1)S(1)} collective-permute-done((bf16[160,512]{1,0:T(8,128)(2,1)}, bf16[160,512]{1,0:T(8,128)(2,1)S(1)}, u32[]{:S(2)}, u32[]{:S(2)}) %collective-permute-start.8) | collective-permute-done | bytes 163872 | tf_op jit(solution)/shard_map/ppermute | solution.py:389
  60.1 1.1 collective-permute-done.9.refs_7_
  61.2 4.0 %shard_map.75 = (bf16[2,128,512]{2,1,0:T(8,128)(2,1)S(1)}, bf16[2,128,512]{2,1,0:T(8,128)(2,1)S(1)}, bf16[2,128,512]{2,1,0:T(8,128)(2,1)S(1)}, bf16[2,128,512]{2,1,0:T(8,128)(2,1)S(1)}) custom-call(s32[8]{0:T(128)S(1)} %get-tuple-element.178.kind_ref, s32[8]{0:T(128)S(1)} %get-tuple-element.177.source_ref, bf16[160,512]{1,0:T(8,128)(2,1)S(1)} %copy-done, ...), custom_call_target="tpu_custom_call" | custom-call | tf_op jit(solution)/shard_map/pallas_call | solution.py:310
  65.3 1.6 collective-permute-start.10
  67.4 5.0 %collective-permute-done.10.refs_3_ = bf16[2,128,512]{2,1,0:T(8,128)(2,1)S(1)} collective-permute-done((bf16[2,128,512]{2,1,0:T(8,128)(2,1)S(1)}, bf16[2,128,512]{2,1,0:T(8,128)(2,1)S(1)}, u32[]{:S(2)}, u32[]{:S(2)}) %collective-permute-start.10) | collective-permute-done | bytes 262176 | tf_op jit(solution)/shard_map/ppermute | solution.py:389
  72.4 6.3 %collective-permute-done.11.refs_4_ = bf16[2,128,512]{2,1,0:T(8,128)(2,1)S(1)} collective-permute-done((bf16[2,128,512]{2,1,0:T(8,128)(2,1)S(1)}, bf16[2,128,512]{2,1,0:T(8,128)(2,1)S(1)}, u32[]{:S(2)}, u32[]{:S(2)}) %collective-permute-start.11) | collective-permute-done | bytes 262176 | tf_op jit(solution)/shard_map/ppermute | solution.py:389
  78.7 0.6 collective-permute-done.12.refs_5_
  79.4 80.6 %shard_map.76 = (bf16[160,512]{1,0:T(8,128)(2,1)S(1)}, bf16[160,512]{1,0:T(8,128)(2,1)S(1)}, bf16[160,512]{1,0:T(8,128)(2,1)S(1)}, bf16[160,512]{1,0:T(8,128)(2,...) custom-call(s32[8]{0:T(128)S(1)} %get-tuple-element.179.order_ref, ...), custom_call_target="tpu_custom_call" | custom-call | flops 23622320128 | bytes 8388608 | tf_op jit(solution)/shard_map/pallas_call | solution.py:339
  160.0 0.7 copy-done.1
  160.6 0.7 copy-done.3
  161.3 0.6 copy-done.4
  161.9 0.7 copy-done.5
  162.6 0.7 copy-done.6
  163.3 0.7 copy-done.7
  163.9 0.7 copy-done.8
  164.6 0.7 copy-done.9
  165.3 0.6 copy-done.10
  165.9 1.5 collective-permute-start.15
  167.3 1.8 collective-permute-done.13.refs_1_
  169.2 0.9 collective-permute-done.14.refs_2_
  170.1 1.5 collective-permute-done.15.refs_3_
  171.6 0.6 copy-done.21
  172.2 2.2 shard_map.77
  174.4 0.8 collective-permute-start.17
  175.3 2.9 collective-permute-start.18
  178.2 1.2 collective-permute-start.20
  180.5 2.4 collective-permute-done.17.refs_2_
  183.0 1.1 conditional.3
  183.0 1.1 broadcast.1044
  184.1 15.2 %collective-permute-done.18.refs_3_ = bf16[160,512]{1,0:T(8,128)(2,1)S(1)} collective-permute-done((bf16[160,512]{1,0:T(8,128)(2,1)}, bf16[160,512]{1,0:T(8,128)(2,1)S(1)}, u32[]{:S(2)}, u32[]{:S(2)}) %collective-permute-start.18) | collective-permute-done | bytes 163872 | tf_op jit(solution)/shard_map/ppermute | solution.py:389
  199.3 3.5 %collective-permute-done.19.refs_4_ = bf16[160,512]{1,0:T(8,128)(2,1)S(1)} collective-permute-done((bf16[160,512]{1,0:T(8,128)(2,1)}, bf16[160,512]{1,0:T(8,128)(2,1)S(1)}, u32[]{:S(2)}, u32[]{:S(2)}) %collective-permute-start.19) | collective-permute-done | bytes 163872 | tf_op jit(solution)/shard_map/ppermute | solution.py:389
  202.8 2.4 collective-permute-done.21.refs_6_
  205.2 2.5 collective-permute-done.22.refs_7_
  207.7 4.0 %shard_map.78 = (bf16[2,128,512]{2,1,0:T(8,128)(2,1)S(1)}, bf16[2,128,512]{2,1,0:T(8,128)(2,1)S(1)}, bf16[2,128,512]{2,1,0:T(8,128)(2,1)S(1)}, bf16[2,128,512]{2,1,0:T(8,128)(2,1)S(1)}) custom-call(s32[8]{0:T(128)S(1)} %get-tuple-element.182.kind_ref, s32[8]{0:T(128)S(1)} %get-tuple-element.181.source_ref, bf16[160,512]{1,0:T(8,128)(2,1)S(1)} %copy-done.2, ...), custom_call_target="tpu_custom_call" | custom-call | tf_op jit(solution)/shard_map/pallas_call | solution.py:310
  211.7 1.0 collective-permute-start.23
  212.7 0.9 collective-permute-start.24
  213.6 4.6 %collective-permute-done.23.refs_3_ = bf16[2,128,512]{2,1,0:T(8,128)(2,1)S(1)} collective-permute-done((bf16[2,128,512]{2,1,0:T(8,128)(2,1)S(1)}, bf16[2,128,512]{2,1,0:T(8,128)(2,1)S(1)}, u32[]{:S(2)}, u32[]{:S(2)}) %collective-permute-start.23) | collective-permute-done | bytes 262176 | tf_op jit(solution)/shard_map/ppermute | solution.py:389
  218.3 6.9 %collective-permute-done.24.refs_4_ = bf16[2,128,512]{2,1,0:T(8,128)(2,1)S(1)} collective-permute-done((bf16[2,128,512]{2,1,0:T(8,128)(2,1)S(1)}, bf16[2,128,512]{2,1,0:T(8,128)(2,1)S(1)}, u32[]{:S(2)}, u32[]{:S(2)}) %collective-permute-start.24) | collective-permute-done | bytes 262176 | tf_op jit(solution)/shard_map/ppermute | solution.py:389
  225.2 0.6 collective-permute-done.25.refs_5_
  225.8 1.9 copy-done.13
  227.7 78.5 %shard_map.79 = bf16[8,128,512]{2,1,0:T(8,128)(2,1)} custom-call(s32[8]{0:T(128)S(1)} %get-tuple-element.180.order_ref, s32[8]{0:T(128)S(1)} %copy-done.11, s32[4]{0:T(128)S(1)} %copy-done.12, bf16[2,128,512]{2,1,0:T(8,128)(2,1)S(1)} %get-tuple-element.157.refs_2_, bf16[2,128,512]{2,1,0:T(8,128)(2,1)S(1)} %collective-permute-done.23.refs_3_, ...), custom_call_target="tpu_custom_call" | custom-call | flops 23622320128 | bytes 8388608 | tf_op jit(solution)/shard_map/pallas_call | solution.py:339
  (121 shorter events, 7.0 us)
Async XLA Ops:
  1.3 14.4 %all-to-all-start.2 = ((s32[32,2,2,8]{3,1,2,0:T(2,128)}), s32[32,2,2,8]{3,1,2,0:T(2,128)S(1)}, u32[]{:S(2)}, u32[]{:S(2)}) async-start(s32[32,2,2,8]{3,1,2,0:T(2,128)} %broadcast_in_dim.246), calls=%async_computation.2 | async-start | bytes 131072 | tf_op jit(solution)/shard_map/all_to_all | solution.py:416
  12.0 12.5 %collective-permute-start = (bf16[32,512]{1,0:T(8,128)(2,1)}, bf16[32,512]{1,0:T(8,128)(2,1)S(1)}, u32[]{:S(2)}, u32[]{:S(2)}) collective-permute-start(bf16[32,512]{1,0:T(8,128)(2,1)} %get-tuple-element.108), channel_id=1, source_target_pairs={{0,8},{4,12},{8,16},{12,20},{16,24},{20,28},{24,0},{28,4},{1,9},{5... | collective-permute-start | bytes 98312 | tf_op jit(solution)/shard_map/ppermute | solution.py:389
  13.2 11.3 %collective-permute-start.1 = (bf16[32,512]{1,0:T(8,128)(2,1)}, bf16[32,512]{1,0:T(8,128)(2,1)S(1)}, u32[]{:S(2)}, u32[]{:S(2)}) collective-permute-start(bf16[32,512]{1,0:T(8,128)(2,1)} %get-tuple-element.109), channel_id=1, source_target_pairs={{0,16},{4,20},{8,24},{12,28},{16,0},{20,4},{24,8},{28,12},{1,17},{... | collective-permute-start | bytes 98312 | tf_op jit(solution)/shard_map/ppermute | solution.py:389
  14.4 10.1 %collective-permute-start.2 = (bf16[32,512]{1,0:T(8,128)(2,1)}, bf16[32,512]{1,0:T(8,128)(2,1)S(1)}, u32[]{:S(2)}, u32[]{:S(2)}) collective-permute-start(bf16[32,512]{1,0:T(8,128)(2,1)} %get-tuple-element.110), channel_id=1, source_target_pairs={{0,24},{4,28},{8,0},{12,4},{16,8},{20,12},{24,16},{28,20},{1,25},{... | collective-permute-start | bytes 98312 | tf_op jit(solution)/shard_map/ppermute | solution.py:389
  24.5 0.6 copy-start.16
  24.5 0.6 copy-start.17
  24.5 0.6 copy-start.18
  27.3 6.0 %collective-permute-start.3 = (bf16[160,512]{1,0:T(8,128)(2,1)}, bf16[160,512]{1,0:T(8,128)(2,1)S(1)}, u32[]{:S(2)}, u32[]{:S(2)}) collective-permute-start(bf16[160,512]{1,0:T(8,128)(2,1)} %get-tuple-element.121), channel_id=1, source_target_pairs={{0,4},{4,8},{8,12},{12,16},{16,20},{20,24},{24,28},{28,0},{1,5},{5... | collective-permute-start | bytes 491528 | tf_op jit(solution)/shard_map/ppermute | solution.py:389
  27.5 8.2 %collective-permute-start.4 = (bf16[160,512]{1,0:T(8,128)(2,1)}, bf16[160,512]{1,0:T(8,128)(2,1)S(1)}, u32[]{:S(2)}, u32[]{:S(2)}) collective-permute-start(bf16[160,512]{1,0:T(8,128)(2,1)} %get-tuple-element.123), channel_id=1, source_target_pairs={{0,8},{4,12},{8,16},{12,20},{16,24},{20,28},{24,0},{28,4},{1,9},{5... | collective-permute-start | bytes 491528 | tf_op jit(solution)/shard_map/ppermute | solution.py:389
  27.9 23.3 %collective-permute-start.5 = (bf16[160,512]{1,0:T(8,128)(2,1)}, bf16[160,512]{1,0:T(8,128)(2,1)S(1)}, u32[]{:S(2)}, u32[]{:S(2)}) collective-permute-start(bf16[160,512]{1,0:T(8,128)(2,1)} %get-tuple-element.124), channel_id=1, source_target_pairs={{0,12},{4,16},{8,20},{12,24},{16,28},{20,0},{24,4},{28,8},{1,13},{... | collective-permute-start | bytes 491528 | tf_op jit(solution)/shard_map/ppermute | solution.py:389
  31.8 23.1 %collective-permute-start.6 = (bf16[160,512]{1,0:T(8,128)(2,1)}, bf16[160,512]{1,0:T(8,128)(2,1)S(1)}, u32[]{:S(2)}, u32[]{:S(2)}) collective-permute-start(bf16[160,512]{1,0:T(8,128)(2,1)} %get-tuple-element.125), channel_id=1, source_target_pairs={{0,16},{4,20},{8,24},{12,28},{16,0},{20,4},{24,8},{28,12},{1,17},{... | collective-permute-start | bytes 491528 | tf_op jit(solution)/shard_map/ppermute | solution.py:389
  31.8 23.1 %collective-permute-start.7 = (bf16[160,512]{1,0:T(8,128)(2,1)}, bf16[160,512]{1,0:T(8,128)(2,1)S(1)}, u32[]{:S(2)}, u32[]{:S(2)}) collective-permute-start(bf16[160,512]{1,0:T(8,128)(2,1)} %get-tuple-element.126), channel_id=1, source_target_pairs={{0,20},{4,24},{8,28},{12,0},{16,4},{20,8},{24,12},{28,16},{1,21},{... | collective-permute-start | bytes 491528 | tf_op jit(solution)/shard_map/ppermute | solution.py:389
  33.3 26.7 %collective-permute-start.8 = (bf16[160,512]{1,0:T(8,128)(2,1)}, bf16[160,512]{1,0:T(8,128)(2,1)S(1)}, u32[]{:S(2)}, u32[]{:S(2)}) collective-permute-start(bf16[160,512]{1,0:T(8,128)(2,1)} %get-tuple-element.127), channel_id=1, source_target_pairs={{0,24},{4,28},{8,0},{12,4},{16,8},{20,12},{24,16},{28,20},{1,25},{... | collective-permute-start | bytes 491528 | tf_op jit(solution)/shard_map/ppermute | solution.py:389
  35.7 25.6 %collective-permute-start.9 = (bf16[160,512]{1,0:T(8,128)(2,1)}, bf16[160,512]{1,0:T(8,128)(2,1)S(1)}, u32[]{:S(2)}, u32[]{:S(2)}) collective-permute-start(bf16[160,512]{1,0:T(8,128)(2,1)} %get-tuple-element.128), channel_id=1, source_target_pairs={{0,28},{4,0},{8,4},{12,8},{16,12},{20,16},{24,20},{28,24},{1,29},{... | collective-permute-start | bytes 491528 | tf_op jit(solution)/shard_map/ppermute | solution.py:389
  36.6 24.6 %copy-start = (bf16[160,512]{1,0:T(8,128)(2,1)S(1)}, bf16[160,512]{1,0:T(8,128)(2,1)}, u32[]{:S(2)}) copy-start(bf16[160,512]{1,0:T(8,128)(2,1)} %get-tuple-element.119.refs_0_) | copy-start | bytes 491524
  36.6 42.7 %copy-start.14 = (bf16[2,512,512]{2,1,0:T(8,128)(2,1)S(1)}, bf16[2,512,512]{2,1,0:T(8,128)(2,1)}, u32[]{:S(2)}) copy-start(bf16[2,512,512]{2,1,0:T(8,128)(2,1)} %refs_8_.3) | copy-start | bytes 3145732
  36.6 42.7 %copy-start.15 = (f32[2,2,512]{2,1,0:T(2,128)S(1)}, f32[2,2,512]{2,1,0:T(2,128)}, u32[]{:S(2)}) copy-start(f32[2,2,512]{2,1,0:T(2,128)} %refs_6_.3) | copy-start | bytes 24580
  65.3 7.1 %collective-permute-start.10 = (bf16[2,128,512]{2,1,0:T(8,128)(2,1)S(1)}, bf16[2,128,512]{2,1,0:T(8,128)(2,1)S(1)}, u32[]{:S(2)}, u32[]{:S(2)}) collective-permute-start(bf16[2,128,512]{2,1,0:T(8,128)(2,1)S(1)} %get-tuple-element.131), channel_id=1, source_target_pairs={{0,1},{1,2},{2,3},{3,0},{4,5},{5,6},{6,7},{7,4},{8,9},{9,10},{10,1... | collective-permute-start | bytes 786440 | tf_op jit(solution)/shard_map/ppermute | solution.py:389
  66.9 11.8 %collective-permute-start.11 = (bf16[2,128,512]{2,1,0:T(8,128)(2,1)S(1)}, bf16[2,128,512]{2,1,0:T(8,128)(2,1)S(1)}, u32[]{:S(2)}, u32[]{:S(2)}) collective-permute-start(bf16[2,128,512]{2,1,0:T(8,128)(2,1)S(1)} %get-tuple-element.132), channel_id=1, source_target_pairs={{0,2},{1,3},{2,0},{3,1},{4,6},{5,7},{6,4},{7,5},{8,10},{9,11},{10,... | collective-permute-start | bytes 786440 | tf_op jit(solution)/shard_map/ppermute | solution.py:389
  67.2 12.2 %collective-permute-start.12 = (bf16[2,128,512]{2,1,0:T(8,128)(2,1)S(1)}, bf16[2,128,512]{2,1,0:T(8,128)(2,1)S(1)}, u32[]{:S(2)}, u32[]{:S(2)}) collective-permute-start(bf16[2,128,512]{2,1,0:T(8,128)(2,1)S(1)} %get-tuple-element.133), channel_id=1, source_target_pairs={{0,3},{1,0},{2,1},{3,2},{4,7},{5,4},{6,5},{7,6},{8,11},{9,8},{10,9... | collective-permute-start | bytes 786440 | tf_op jit(solution)/shard_map/ppermute | solution.py:389
  159.9 0.7 copy-start.1
  160.6 0.7 copy-start.3
  161.3 0.7 copy-start.4
  161.9 0.7 copy-start.5
  162.6 0.7 copy-start.6
  163.3 0.7 copy-start.7
  163.9 0.7 copy-start.8
  164.6 0.7 copy-start.9
  165.3 0.6 copy-start.10
  165.9 3.3 %collective-permute-start.13 = (bf16[32,512]{1,0:T(8,128)(2,1)S(1)}, bf16[32,512]{1,0:T(8,128)(2,1)S(1)}, u32[]{:S(2)}, u32[]{:S(2)}) collective-permute-start(bf16[32,512]{1,0:T(8,128)(2,1)S(1)} %get-tuple-element.135), channel_id=1, source_target_pairs={{0,8},{4,12},{8,16},{12,20},{16,24},{20,28},{24,0},{28,4},{1,9},{5... | collective-permute-start | bytes 98312 | tf_op jit(solution)/shard_map/ppermute | solution.py:389
  165.9 4.2 %collective-permute-start.14 = (bf16[32,512]{1,0:T(8,128)(2,1)S(1)}, bf16[32,512]{1,0:T(8,128)(2,1)S(1)}, u32[]{:S(2)}, u32[]{:S(2)}) collective-permute-start(bf16[32,512]{1,0:T(8,128)(2,1)S(1)} %get-tuple-element.136), channel_id=1, source_target_pairs={{0,16},{4,20},{8,24},{12,28},{16,0},{20,4},{24,8},{28,12},{1,17},{... | collective-permute-start | bytes 98312 | tf_op jit(solution)/shard_map/ppermute | solution.py:389
  165.9 5.7 %collective-permute-start.15 = (bf16[32,512]{1,0:T(8,128)(2,1)S(1)}, bf16[32,512]{1,0:T(8,128)(2,1)S(1)}, u32[]{:S(2)}, u32[]{:S(2)}) collective-permute-start(bf16[32,512]{1,0:T(8,128)(2,1)S(1)} %get-tuple-element.137), channel_id=1, source_target_pairs={{0,24},{4,28},{8,0},{12,4},{16,8},{20,12},{24,16},{28,20},{1,25},{... | collective-permute-start | bytes 98312 | tf_op jit(solution)/shard_map/ppermute | solution.py:389
  169.2 2.4 copy-start.19
  170.1 1.5 copy-start.20
  171.6 0.6 copy-start.21
  174.4 5.6 %collective-permute-start.16 = (bf16[160,512]{1,0:T(8,128)(2,1)}, bf16[160,512]{1,0:T(8,128)(2,1)S(1)}, u32[]{:S(2)}, u32[]{:S(2)}) collective-permute-start(bf16[160,512]{1,0:T(8,128)(2,1)} %get-tuple-element.148), channel_id=1, source_target_pairs={{0,4},{4,8},{8,12},{12,16},{16,20},{20,24},{24,28},{28,0},{1,5},{5... | collective-permute-start | bytes 491528 | tf_op jit(solution)/shard_map/ppermute | solution.py:389
  174.4 8.4 %collective-permute-start.17 = (bf16[160,512]{1,0:T(8,128)(2,1)}, bf16[160,512]{1,0:T(8,128)(2,1)S(1)}, u32[]{:S(2)}, u32[]{:S(2)}) collective-permute-start(bf16[160,512]{1,0:T(8,128)(2,1)} %get-tuple-element.150), channel_id=1, source_target_pairs={{0,8},{4,12},{8,16},{12,20},{16,24},{20,28},{24,0},{28,4},{1,9},{5... | collective-permute-start | bytes 491528 | tf_op jit(solution)/shard_map/ppermute | solution.py:389
  175.3 24.0 %collective-permute-start.18 = (bf16[160,512]{1,0:T(8,128)(2,1)}, bf16[160,512]{1,0:T(8,128)(2,1)S(1)}, u32[]{:S(2)}, u32[]{:S(2)}) collective-permute-start(bf16[160,512]{1,0:T(8,128)(2,1)} %get-tuple-element.151), channel_id=1, source_target_pairs={{0,12},{4,16},{8,20},{12,24},{16,28},{20,0},{24,4},{28,8},{1,13},{... | collective-permute-start | bytes 491528 | tf_op jit(solution)/shard_map/ppermute | solution.py:389
  178.2 24.6 %collective-permute-start.19 = (bf16[160,512]{1,0:T(8,128)(2,1)}, bf16[160,512]{1,0:T(8,128)(2,1)S(1)}, u32[]{:S(2)}, u32[]{:S(2)}) collective-permute-start(bf16[160,512]{1,0:T(8,128)(2,1)} %get-tuple-element.152), channel_id=1, source_target_pairs={{0,16},{4,20},{8,24},{12,28},{16,0},{20,4},{24,8},{28,12},{1,17},{... | collective-permute-start | bytes 491528 | tf_op jit(solution)/shard_map/ppermute | solution.py:389
  178.2 24.6 %collective-permute-start.20 = (bf16[160,512]{1,0:T(8,128)(2,1)}, bf16[160,512]{1,0:T(8,128)(2,1)S(1)}, u32[]{:S(2)}, u32[]{:S(2)}) collective-permute-start(bf16[160,512]{1,0:T(8,128)(2,1)} %get-tuple-element.153), channel_id=1, source_target_pairs={{0,20},{4,24},{8,28},{12,0},{16,4},{20,8},{24,12},{28,16},{1,21},{... | collective-permute-start | bytes 491528 | tf_op jit(solution)/shard_map/ppermute | solution.py:389
  180.0 25.2 %collective-permute-start.21 = (bf16[160,512]{1,0:T(8,128)(2,1)}, bf16[160,512]{1,0:T(8,128)(2,1)S(1)}, u32[]{:S(2)}, u32[]{:S(2)}) collective-permute-start(bf16[160,512]{1,0:T(8,128)(2,1)} %get-tuple-element.154), channel_id=1, source_target_pairs={{0,24},{4,28},{8,0},{12,4},{16,8},{20,12},{24,16},{28,20},{1,25},{... | collective-permute-start | bytes 491528 | tf_op jit(solution)/shard_map/ppermute | solution.py:389
  182.8 24.8 %collective-permute-start.22 = (bf16[160,512]{1,0:T(8,128)(2,1)}, bf16[160,512]{1,0:T(8,128)(2,1)S(1)}, u32[]{:S(2)}, u32[]{:S(2)}) collective-permute-start(bf16[160,512]{1,0:T(8,128)(2,1)} %get-tuple-element.155), channel_id=1, source_target_pairs={{0,28},{4,0},{8,4},{12,8},{16,12},{20,16},{24,20},{28,24},{1,29},{... | collective-permute-start | bytes 491528 | tf_op jit(solution)/shard_map/ppermute | solution.py:389
  183.0 24.7 %copy-start.2 = (bf16[160,512]{1,0:T(8,128)(2,1)S(1)}, bf16[160,512]{1,0:T(8,128)(2,1)}, u32[]{:S(2)}) copy-start(bf16[160,512]{1,0:T(8,128)(2,1)} %get-tuple-element.146.refs_0_) | copy-start | bytes 491524
  183.0 42.8 %copy-start.11 = (s32[8]{0:T(128)S(1)}, s32[8]{0:T(128)}, u32[]{:S(2)}) copy-start(s32[8]{0:T(128)} %get-tuple-element.214.pick_ref.refs_0_) | copy-start | bytes 100
  183.0 42.8 %copy-start.12 = (s32[4]{0:T(128)S(1)}, s32[4]{0:T(128)}, u32[]{:S(2)}) copy-start(s32[4]{0:T(128)} %get-tuple-element.212.spare_ref.refs_1_) | copy-start | bytes 52
  211.7 6.5 %collective-permute-start.23 = (bf16[2,128,512]{2,1,0:T(8,128)(2,1)S(1)}, bf16[2,128,512]{2,1,0:T(8,128)(2,1)S(1)}, u32[]{:S(2)}, u32[]{:S(2)}) collective-permute-start(bf16[2,128,512]{2,1,0:T(8,128)(2,1)S(1)} %get-tuple-element.158), channel_id=1, source_target_pairs={{0,1},{1,2},{2,3},{3,0},{4,5},{5,6},{6,7},{7,4},{8,9},{9,10},{10,1... | collective-permute-start | bytes 786440 | tf_op jit(solution)/shard_map/ppermute | solution.py:389
  212.7 12.5 %collective-permute-start.24 = (bf16[2,128,512]{2,1,0:T(8,128)(2,1)S(1)}, bf16[2,128,512]{2,1,0:T(8,128)(2,1)S(1)}, u32[]{:S(2)}, u32[]{:S(2)}) collective-permute-start(bf16[2,128,512]{2,1,0:T(8,128)(2,1)S(1)} %get-tuple-element.159), channel_id=1, source_target_pairs={{0,2},{1,3},{2,0},{3,1},{4,6},{5,7},{6,4},{7,5},{8,10},{9,11},{10,... | collective-permute-start | bytes 786440 | tf_op jit(solution)/shard_map/ppermute | solution.py:389
  213.6 12.2 %collective-permute-start.25 = (bf16[2,128,512]{2,1,0:T(8,128)(2,1)S(1)}, bf16[2,128,512]{2,1,0:T(8,128)(2,1)S(1)}, u32[]{:S(2)}, u32[]{:S(2)}) collective-permute-start(bf16[2,128,512]{2,1,0:T(8,128)(2,1)S(1)} %get-tuple-element.160), channel_id=1, source_target_pairs={{0,3},{1,0},{2,1},{3,2},{4,7},{5,4},{6,5},{7,6},{8,11},{9,8},{10,9... | collective-permute-start | bytes 786440 | tf_op jit(solution)/shard_map/ppermute | solution.py:389
  225.8 1.9 copy-start.13

commit v3 on v2

--- a/solution.py
+++ b/solution.py
@@ -13,10 +13,11 @@
 LAYERS = 2
 LANES = 128
 WAYS = 4
+TAG_ROWS = 16
 FF_BLOCK = 512
 BF16 = jnp.bfloat16
 F32 = jnp.float32
-HBM = pl.BlockSpec(memory_space=pltpu.HBM)
+HBM = pl.BlockSpec(memory_space=pl.ANY)
 SMEM = pl.BlockSpec(memory_space=pltpu.SMEM)
 VMEM = pl.BlockSpec(memory_space=pltpu.VMEM)
 
@@ -39,7 +40,7 @@
     copy.wait()
 
 
-def send_bricks(action, patch, bricks, tables, payload, spare, hops, sems):
+def send_bricks(action, patch, bricks, tables, payload, spare, hops, sems, tag=None):
     pick_ref, spare_ref = tables
     size, rows, width = bricks.shape
     peers = len(payload)
@@ -73,37 +74,52 @@
         tall = rows // len(hops)
         for way in range(len(hops)):
             window = pl.ds(way * tall, tall)
-            action(pltpu.make_async_copy(source.at[window], hops[way], sems.at[2, way]))
-
-
-def pack_kernel(pick_ref, spare_ref, points, *refs):
+            target = hops[way].at[pl.ds(0, tall)]
+            action(pltpu.make_async_copy(source.at[window], target, sems.at[2, way]))
+
+    if tag is not None:
+        tall = hops[0].shape[0] - TAG_ROWS
+        for way in range(len(hops)):
+            target = hops[way].at[pl.ds(tall, TAG_ROWS), pl.ds(0, LANES)]
+            action(pltpu.make_async_copy(tag, target, sems.at[3, way]))
+
+
+def pack_kernel(pick_ref, spare_ref, tag, points, *refs):
     peers = pick_ref.shape[0]
     payload, spare, hops, sems = refs[:peers], refs[peers], refs[peers + 1 : -1], refs[-1]
     for action in (start, wait):
-        send_bricks(action, 0, points, (pick_ref, spare_ref), payload, spare, hops, sems)
-
-
-def relay_kernel(ways, relay_ref, *refs):
-    peers = relay_ref.shape[0]
+        send_bricks(action, 0, points, (pick_ref, spare_ref), payload, spare, hops, sems, tag)
+
+
+def relay_kernel(ways, tagged, goal_ref, *refs):
+    peers = (len(refs) - 4 - ways) // 2
     hops, payload = refs[:ways], refs[ways + peers : ways + 2 * peers]
-    staged, in_sems, out_sems = refs[ways + 2 * peers :]
+    staged, tags, in_sems, out_sems = refs[ways + 2 * peers :]
     _, tall, _ = staged.shape
     rows = payload[0].shape[0] - tall
     for action in (start, wait):
         for way in range(ways):
-            action(pltpu.make_async_copy(hops[way], staged.at[way], in_sems.at[way]))
+            source = hops[way].at[pl.ds(0, tall)]
+            action(pltpu.make_async_copy(source, staged.at[way], in_sems.at[0, way]))
+            if tagged:
+                source = hops[way].at[pl.ds(tall, TAG_ROWS), pl.ds(0, LANES)]
+                action(pltpu.make_async_copy(source, tags.at[way], in_sems.at[1, way]))
+    goals = []
+    for way in range(ways):
+        if tagged:
+            tag = jnp.max(tags[way].astype(F32)).astype(jnp.int32)
+            ahead = (tag - 1 - way * (peers // ways) + peers) % peers
+            goals.append(jnp.where(tag > 0, ahead, -1))
+        else:
+            goals.append(goal_ref[way])
     for action in (start, wait):
-        for shift in range(peers):
-
-            @pl.when(relay_ref[shift] >= 0)
-            def _():
-                action(
-                    pltpu.make_async_copy(
-                        staged.at[relay_ref[shift]],
-                        payload[shift].at[pl.ds(rows, tall)],
-                        out_sems.at[shift],
-                    )
-                )
+        for way in range(ways):
+            for shift in range(peers):
+
+                @pl.when(goals[way] == shift)
+                def _():
+                    target = payload[shift].at[pl.ds(rows, tall)]
+                    action(pltpu.make_async_copy(staged.at[way], target, out_sems.at[way]))
 
 
 def turn_kernel(peers, kind_ref, source_ref, *refs):
@@ -146,17 +162,31 @@
         pltpu.make_async_copy(extra.at[slot], out, out_sems.at[slot]).wait()
 
 
-def attend(q_ref, k_ref, v_ref, mixed_ref):
+def attend(q_ref, k_ref, v_ref, mixed_ref, shifted):
     tiles, count, _ = v_ref.shape
     head_of = lax.broadcasted_iota(jnp.int32, (count, LANES), 1) // HEAD_DIM
     per_tile = LANES // HEAD_DIM
 
-    def weigh(queries, keys, values, head, shifted):
+    def weigh(queries, keys, values, head):
         chosen = jnp.where(head_of == head, queries, jnp.zeros_like(queries))
         scores = matmul(chosen, keys, ((1,), (1,)))
         if shifted:
             scores = scores - jnp.max(scores, axis=1, keepdims=True)
         return matmul(jnp.exp2(scores).astype(BF16), values)
+
+    if shifted:
+
+        @pl.loop(0, tiles)
+        def _(tile):
+            column = pl.ds(pl.multiple_of(tile * LANES, LANES), LANES)
+
+            @pl.loop(0, per_tile)
+            def _(head):
+                sums = weigh(q_ref[:, column], k_ref[:, column], v_ref[tile], head)
+                mixed = (sums[:, :LANES] / sums[:, LANES:]).astype(BF16)
+                mixed_ref[:, column] = jnp.where(head_of == head, mixed, mixed_ref[:, column])
+
+        return None
 
     low = jnp.full((count, LANES), 1.0, F32)
     high = jnp.full((count, LANES), 1.0, F32)
@@ -166,25 +196,13 @@
         above = jnp.zeros((count, LANES), F32)
         below = jnp.ones((count, LANES), F32)
         for head in range(per_tile):
-            sums = weigh(queries, keys, values, head, False)
+            sums = weigh(queries, keys, values, head)
             above = jnp.where(head_of == head, sums[:, :LANES], above)
             below = jnp.where(head_of == head, sums[:, LANES:], below)
         mixed_ref[:, column] = (above / below).astype(BF16)
         low = jnp.minimum(low, below)
         high = jnp.maximum(high, below)
-    safe = (jnp.min(low) > 2.0**-60) & (jnp.max(high) < 2.0**100)
-
-    @pl.when(jnp.logical_not(safe))
-    def _():
-        @pl.loop(0, tiles)
-        def _(tile):
-            column = pl.ds(pl.multiple_of(tile * LANES, LANES), LANES)
-
-            @pl.loop(0, per_tile)
-            def _(head):
-                sums = weigh(q_ref[:, column], k_ref[:, column], v_ref[tile], head, True)
-                mixed = (sums[:, :LANES] / sums[:, LANES:]).astype(BF16)
-                mixed_ref[:, column] = jnp.where(head_of == head, mixed, mixed_ref[:, column])
+    return (jnp.min(low) > 2.0**-60) & (jnp.max(high) < 2.0**100)
 
 
 def layer_kernel(layer, columns, peers, order_ref, *refs):
@@ -246,20 +264,29 @@
     for tile in range(width // LANES):
         v_ref[tile, :, :LANES] = values[:, tile * LANES : (tile + 1) * LANES]
 
-    attend(q_ref, k_ref, v_ref, mixed_ref)
-
     arrive(1)
-    mixed = (x.astype(F32) + matmul(mixed_ref[...], wout_ref[...])).astype(BF16)
-    inner = normalize(mixed.astype(F32), gain_ref[layer, 1:2, :]).astype(BF16)
-    total = mixed.astype(F32)
     arrive(2)
     arrive(3)
-    for begin in range(0, wup_ref.shape[1], FF_BLOCK):
-        up = matmul(inner, wup_ref[:, begin : begin + FF_BLOCK])
-        half = up * 0.5
-        hidden = (half + half * lax.erf(up * math.sqrt(0.5))).astype(BF16)
-        total = total + matmul(hidden, wdown_ref[begin : begin + FF_BLOCK, :])
-    y_ref[turn] = total.astype(BF16).reshape(per_patch, rows, width)
+
+    def finish(shifted):
+        safe = attend(q_ref, k_ref, v_ref, mixed_ref, shifted)
+        mixed = (x.astype(F32) + matmul(mixed_ref[...], wout_ref[...])).astype(BF16)
+        inner = normalize(mixed.astype(F32), gain_ref[layer, 1:2, :]).astype(BF16)
+        total = mixed.astype(F32)
+        for begin in range(0, wup_ref.shape[1], FF_BLOCK):
+            up = matmul(inner, wup_ref[:, begin : begin + FF_BLOCK])
+            half = up * 0.5
+            hidden = (half + half * lax.erf(up * math.sqrt(0.5))).astype(BF16)
+            total = total + matmul(hidden, wdown_ref[begin : begin + FF_BLOCK, :])
+        y_ref[turn] = total.astype(BF16).reshape(per_patch, rows, width)
+        return safe
+
+    safe = finish(False)
+
+    @pl.when(jnp.logical_not(safe))
+    def _():
+        finish(True)
+
     store(start, turn)
 
     @pl.when(turn == patches - 1)
@@ -268,40 +295,44 @@
             store(wait, step)
 
 
-def send_shapes(count, rows, width, peers):
+def send_shapes(count, rows, width, peers, tag_rows=0):
     tall = rows // WAYS
     shapes = [jax.ShapeDtypeStruct((rows + tall, width), BF16)] * peers
     shapes += [jax.ShapeDtypeStruct((max(1, count // 2), rows, width), BF16)]
-    return shapes + [jax.ShapeDtypeStruct((tall, width), BF16)] * WAYS
-
-
-def pack(points, tables):
+    return shapes + [jax.ShapeDtypeStruct((tall + tag_rows, width), BF16)] * WAYS
+
+
+def pack(points, tag, tables):
     count, rows, width = points.shape
     peers = tables[0].shape[0]
-    shapes = send_shapes(count, rows, width, peers)
+    shapes = send_shapes(count, rows, width, peers, TAG_ROWS)
     return pl.pallas_call(
         pack_kernel,
-        in_specs=[SMEM] * 2 + [VMEM],
+        in_specs=[SMEM] * 2 + [VMEM] * 2,
         out_specs=[HBM] * len(shapes),
         out_shape=shapes,
-        scratch_shapes=[pltpu.SemaphoreType.DMA((3, max(peers, count)))],
-    )(*tables, points)
-
-
-def relay(picks, hops, payload):
-    peers = len(payload)
+        scratch_shapes=[pltpu.SemaphoreType.DMA((4, max(peers, count)))],
+        compiler_params=pltpu.CompilerParams(vmem_limit_bytes=8 * 2**20),
+    )(*tables, tag, points)
+
+
+def relay(goals, hops, payload):
+    peers, ways = len(payload), len(hops)
+    tall = payload[0].shape[0] // (WAYS + 1)
     return pl.pallas_call(
-        functools.partial(relay_kernel, len(hops)),
-        in_specs=[SMEM] + [HBM] * (len(hops) + peers),
+        functools.partial(relay_kernel, ways, hops[0].shape[0] > tall),
+        in_specs=[SMEM] + [HBM] * (ways + peers),
         out_specs=[HBM] * peers,
         out_shape=[jax.ShapeDtypeStruct(slot.shape, BF16) for slot in payload],
-        input_output_aliases={1 + len(hops) + i: i for i in range(peers)},
+        input_output_aliases={1 + ways + i: i for i in range(peers)},
         scratch_shapes=[
-            pltpu.VMEM((len(hops),) + hops[0].shape, BF16),
-            pltpu.SemaphoreType.DMA((len(hops),)),
-            pltpu.SemaphoreType.DMA((peers,)),
+            pltpu.VMEM((ways, tall, payload[0].shape[1]), BF16),
+            pltpu.VMEM((ways, TAG_ROWS, LANES), BF16),
+            pltpu.SemaphoreType.DMA((2, ways)),
+            pltpu.SemaphoreType.DMA((ways,)),
         ],
-    )(picks, *hops, *payload)
+        compiler_params=pltpu.CompilerParams(vmem_limit_bytes=8 * 2**20),
+    )(goals, *hops, *payload)
 
 
 def turn_bricks(kind, source, arrived, second, columns):
@@ -318,7 +349,7 @@
             pltpu.SemaphoreType.DMA((peers + slots,)),
             pltpu.SemaphoreType.DMA((slots,)),
         ],
-        compiler_params=pltpu.CompilerParams(vmem_limit_bytes=32 * 2**20),
+        compiler_params=pltpu.CompilerParams(vmem_limit_bytes=16 * 2**20),
     )(kind, source, *arrived, second)
 
 
@@ -377,11 +408,6 @@
     return jnp.sum(jnp.where(hit, found[..., None, :], 0), axis=-1)
 
 
-def most(keys, values, chosen):
-    hit = (keys[..., None, :] == values[:, None]) & chosen[..., None, :]
-    return jnp.max(jnp.sum(hit.astype(jnp.int32), axis=-1))
-
-
 def shifted(arrays, axis):
     size = lax.axis_size(axis)
     step = size // len(arrays)
@@ -413,50 +439,59 @@
     across_slot = across * room + ranks(across)
     tables = [(pick[layer], spare[layer]) for layer in range(LAYERS)]
 
-    everyone = swap(jnp.broadcast_to(moved_to[None], (devices,) + moved_to.shape), ("gx", "gy"))
-    targets = everyone[:, :, 0] // count // columns
-    behind = ranks(targets) > 0
-    opening = behind & (jnp.cumsum(behind.astype(jnp.int32), axis=-1) == 1)
-    relayed = jnp.sum(jnp.where(opening, targets + 1, 0), axis=-1) - 1
-    flat = lambda values: values.transpose(1, 0, 2).reshape(LAYERS, total)
-    first, second = flat(everyone[:, :, 0]), flat(everyone[:, :, 1])
-    behind = flat(behind)
-    owner = jnp.arange(total) // count
-
-    def crowded(layer):
-        out = jnp.sum(behind[layer].reshape(devices, count).astype(jnp.int32), axis=1)
-        return (jnp.max(out) > 1) | (
-            most(first[layer] // count, jnp.arange(devices), behind[layer]) > 1
+    def plan_all(moved_to):
+        everyone = swap(jnp.broadcast_to(moved_to[None], (devices,) + moved_to.shape), ("gx", "gy"))
+        targets = everyone[:, :, 0] // count // columns
+        behind = ranks(targets) > 0
+        opening = behind & (jnp.cumsum(behind.astype(jnp.int32), axis=-1) == 1)
+        relayed = jnp.sum(jnp.where(opening, targets + 1, 0), axis=-1) - 1
+        flat = lambda values: values.transpose(1, 0, 2).reshape(LAYERS, total)
+        first, second = flat(everyone[:, :, 0]), flat(everyone[:, :, 1])
+        behind = flat(behind)
+        owner = jnp.arange(total) // count
+
+        devs = jnp.arange(devices)
+        lands = (first // count)[:, None, :] == devs[:, None]
+        sends = owner[None, None, :] == devs[:, None]
+        counts = jnp.sum(
+            (jnp.stack([lands, jnp.broadcast_to(sends, lands.shape)]) & behind[:, None, :]).astype(
+                jnp.int32
+            ),
+            axis=-1,
         )
-
-    across_rank = flat(ranks(everyone[:, :, 1] // count % columns))
-    mine = me * count + bricks
-    slots = jnp.arange(columns * room)
-    every = jnp.arange(devices)
-    in_column = every % columns == column
-    plans = []
+        extra = jnp.max(counts) > 1
+
+        across_rank = flat(ranks(everyone[:, :, 1] // count % columns))
+        mine = me * count + bricks
+        slots = jnp.arange(columns * room)
+        every = jnp.arange(devices)
+        in_column = every % columns == column
+        plans = []
+        for layer in range(LAYERS):
+            goal = jnp.where(relayed[:, layer] >= 0, (relayed[:, layer] - row) % peers, -1)
+            behind_me = jnp.where(in_column, (row - every // columns) % peers, -1)
+            goals = lookup(behind_me, jnp.arange(WAYS) * stride, goal)
+            origin = lookup(first[layer], mine, (row - owner // columns) % peers)
+            kind = lookup(first[layer], mine, jnp.where(behind[layer], jnp.where(extra, 2, 1), 0))
+            slot_kind = lookup(across_slot[layer], slots, kind)
+            slot_origin = lookup(across_slot[layer], slots, origin)
+            order = lookup(
+                second[layer], mine, (column - owner % columns) % columns * room + across_rank[layer]
+            )
+            plans.append((extra, goals, slot_kind, slot_origin, order))
+        return plans
+
+    goal = jnp.sum(jnp.where(place[0] == 0, ahead[0] + 1, 0))
+    tag = jnp.broadcast_to(goal.astype(BF16), (TAG_ROWS, LANES))
+    made = pack(points, tag, tables[0])
+    plans = plan_all(moved_to)
     for layer in range(LAYERS):
-        extra = crowded(layer)
-        goal = jnp.where(in_column & (relayed[:, layer] >= 0), (relayed[:, layer] - row) % peers, -1)
-        behind_me = (row - every // columns) % peers
-        hit = (goal[None, :] == shifts[:, None]) & (behind_me % stride == 0)[None, :]
-        relays = jnp.max(jnp.where(hit, behind_me[None, :] // stride, -1), axis=1)
-        origin = lookup(first[layer], mine, (row - owner // columns) % peers)
-        kind = lookup(first[layer], mine, jnp.where(behind[layer], jnp.where(extra, 2, 1), 0))
-        slot_kind = lookup(across_slot[layer], slots, kind)
-        slot_origin = lookup(across_slot[layer], slots, origin)
-        order = lookup(
-            second[layer], mine, (column - owner % columns) % columns * room + across_rank[layer]
-        )
-        plans.append((extra, relays, slot_kind, slot_origin, order))
-
-    made = pack(points, tables[0])
-    for layer in range(LAYERS):
-        extra, relays, slot_kind, slot_origin, order = plans[layer]
         payload, spares, hops = made[:peers], made[peers], made[peers + 1 :]
         hops = shifted(hops, "gx")
-        payload = relay(relays, hops, payload)
+        goals = plans[layer][1] if layer else jnp.zeros((WAYS,), jnp.int32)
+        payload = list(relay(goals, hops, payload))
         arrived = shifted(payload, "gx")
+        extra, _, slot_kind, slot_origin, order = plans[layer]
 
         def send_second(spares, layer=layer):
             target = (ahead[layer] + row) % peers

time: 307 us -> 318 us (1.036)
  Pallas kernels: 174 us -> 198 us
  local copies, waits for them, and re-layouts: 15.2 us -> 8.5 us
    pallas_call x2, Pallas kernels: 159 us -> 185 us  [encoder_layer(): pl.pallas_call(functools.partial(layer_kernel, layer, columns, peers), gr...]
    unnamed x48 -> x12, local copies, waits for them, and re-layouts: 9.94 us -> 4.04 us
  transfers between devices with their start and end apart: 27 -> 27, of which waited for: 20 -> 20; matrix products, arithmetic and copies ran while one was open for 3% -> 2% of each run, Pallas kernels for 1% -> 1%
where the time goes in v3:
time: 318 us; the launch traced here: 319 us
  Pallas kernels  198 us (62%)
  waiting for transfers between devices  77.9 us (24%)
  starting transfers between devices  29.4 us (9%)
  local copies, waits for them, and re-layouts  8.5 us (3%)
  other arithmetic  3.59 us (1%)
    pallas_call x2, Pallas kernels, encoder_layer(): pl.pallas_call(functools.partial(layer_kernel, layer, columns, peers), gr...  185 us
    ppermute x26, waiting for transfers between devices, shifted(): lax.ppermute(arrays[d], axis, [(i, (i + d * step) % size) for i in range(...  77.9 us
    ppermute x26, starting transfers between devices, shifted(): lax.ppermute(arrays[d], axis, [(i, (i + d * step) % size) for i in range(...  23.1 us
    pallas_call x2, Pallas kernels, turn_bricks(): pl.pallas_call(functools.partial(turn_kernel, peers), in_specs=[SMEM] * 2...  8.1 us
  transfers between devices with their start and end apart: 27, of which 20 were waited for; matrix products, arithmetic and copies ran while one was open for 2% of the time, Pallas kernels for 1%

profile of v3, /device:TPU:13, one launch (start us, length us, event | category | flops | bytes accessed | tf_op | source)
XLA Modules:
  0.0 319.4 jit_solution(5908065232039095890)
XLA Ops:
  0.0 0.7 copy.48
  0.7 0.6 broadcast_in_dim.235
  1.3 6.3 %all-to-all-start.2 = ((s32[32,2,2,8]{3,1,2,0:T(2,128)}), s32[32,2,2,8]{3,1,2,0:T(2,128)S(1)}, u32[]{:S(2)}, u32[]{:S(2)}) async-start(s32[32,2,2,8]{3,1,2,0:T(2,128)} %broadcast_in_dim.235), calls=%async_computation.2 | async-start | bytes 131072 | tf_op jit(solution)/shard_map/all_to_all | solution.py:443
  7.7 0.2 convert_reduce_fusion.3
  8.0 0.2 reduce_window_sum.22
  8.2 0.7 fusion.40
  8.9 0.1 select_reduce_fusion.10
  9.0 0.2 select_reduce_fusion.4
  9.9 1.2 copy-done
  11.2 2.7 shard_map.73
  13.9 1.3 collective-permute-start
  15.1 1.2 collective-permute-start.1
  16.3 1.3 collective-permute-start.2
  18.4 0.2 convert_reduce_fusion
  18.6 0.6 reduce_max.9
  21.5 1.4 shard_map.74
  22.9 1.5 collective-permute-start.4
  24.4 0.2 fusion.9
  24.7 2.8 collective-permute-start.5
  27.5 1.5 collective-permute-start.7
  29.0 2.0 collective-permute-start.8
  31.1 0.3 collective-permute-start.9
  31.4 0.1 select_reduce_fusion.6
  31.7 1.1 conditional.2
  31.8 1.1 broadcast.928
  32.8 13.6 %collective-permute-done.5.refs_3_ = bf16[160,512]{1,0:T(8,128)(2,1)S(1)} collective-permute-done((bf16[160,512]{1,0:T(8,128)(2,1)S(1)}, bf16[160,512]{1,0:T(8,128)(2,1)S(1)}, u32[]{:S(2)}, u32[]{:S(2)}) %collective-permute-start.5) | collective-permute-done | bytes 163872 | tf_op jit(solution)/shard_map/ppermute | solution.py:415
  46.4 3.5 %collective-permute-done.6.refs_4_ = bf16[160,512]{1,0:T(8,128)(2,1)S(1)} collective-permute-done((bf16[160,512]{1,0:T(8,128)(2,1)S(1)}, bf16[160,512]{1,0:T(8,128)(2,1)S(1)}, u32[]{:S(2)}, u32[]{:S(2)}) %collective-permute-start.6) | collective-permute-done | bytes 163872 | tf_op jit(solution)/shard_map/ppermute | solution.py:415
  50.0 5.3 %collective-permute-done.8.refs_6_ = bf16[160,512]{1,0:T(8,128)(2,1)S(1)} collective-permute-done((bf16[160,512]{1,0:T(8,128)(2,1)S(1)}, bf16[160,512]{1,0:T(8,128)(2,1)S(1)}, u32[]{:S(2)}, u32[]{:S(2)}) %collective-permute-start.8) | collective-permute-done | bytes 163872 | tf_op jit(solution)/shard_map/ppermute | solution.py:415
  55.3 1.1 collective-permute-done.9.refs_7_
  56.4 4.0 %shard_map.75 = (bf16[2,128,512]{2,1,0:T(8,128)(2,1)S(1)}, bf16[2,128,512]{2,1,0:T(8,128)(2,1)S(1)}, bf16[2,128,512]{2,1,0:T(8,128)(2,1)S(1)}, bf16[2,128,512]{2,1,0:T(8,128)(2,1)S(1)}) custom-call(s32[8]{0:T(128)S(1)} %get-tuple-element.170.kind_ref, s32[8]{0:T(128)S(1)} %get-tuple-element.169.source_ref, bf16[160,512]{1,0:T(8,128)(2,1)S(1)} %get-tuple-element.119.refs_0_, ...), custom_call_target="tpu_custom_call" | custom-call | tf_op jit(solution)/shard_map/pallas_call | solution.py:341
  60.4 1.6 collective-permute-start.10
  62.1 0.3 collective-permute-start.11
  62.3 0.2 collective-permute-start.12
  62.7 4.9 %collective-permute-done.10.refs_3_ = bf16[2,128,512]{2,1,0:T(8,128)(2,1)S(1)} collective-permute-done((bf16[2,128,512]{2,1,0:T(8,128)(2,1)S(1)}, bf16[2,128,512]{2,1,0:T(8,128)(2,1)S(1)}, u32[]{:S(2)}, u32[]{:S(2)}) %collective-permute-start.10) | collective-permute-done | bytes 262176 | tf_op jit(solution)/shard_map/ppermute | solution.py:415
  67.6 6.3 %collective-permute-done.11.refs_4_ = bf16[2,128,512]{2,1,0:T(8,128)(2,1)S(1)} collective-permute-done((bf16[2,128,512]{2,1,0:T(8,128)(2,1)S(1)}, bf16[2,128,512]{2,1,0:T(8,128)(2,1)S(1)}, u32[]{:S(2)}, u32[]{:S(2)}) %collective-permute-start.11) | collective-permute-done | bytes 262176 | tf_op jit(solution)/shard_map/ppermute | solution.py:415
  73.9 0.6 collective-permute-done.12.refs_5_
  74.5 99.5 %shard_map.76 = (bf16[160,512]{1,0:T(8,128)(2,1)S(1)}, bf16[160,512]{1,0:T(8,128)(2,1)S(1)}, bf16[160,512]{1,0:T(8,128)(2,1)S(1)}, bf16[160,512]{1,0:T(8,128)(2,...) custom-call(s32[8]{0:T(128)S(1)} %get-tuple-element.171.order_ref, ...), custom_call_target="tpu_custom_call" | custom-call | flops 23622320128 | bytes 8388608 | tf_op jit(solution)/shard_map/pallas_call | solution.py:370
  174.2 1.4 collective-permute-start.15
  175.6 0.2 select_reduce_fusion.11.goal_ref
  175.8 1.6 collective-permute-done.13.refs_1_
  177.4 1.0 collective-permute-done.14.refs_2_
  178.3 1.5 collective-permute-done.15.refs_3_
  179.9 1.2 shard_map.77
  181.2 0.6 collective-permute-start.17
  181.8 3.1 collective-permute-start.18
  184.9 1.2 collective-permute-start.20
  186.1 0.3 collective-permute-done.16.refs_1_
  186.5 0.7 collective-permute-start.21
  187.2 2.1 collective-permute-done.17.refs_2_
  189.3 0.1 select_reduce_fusion.8
  189.5 1.1 conditional.3
  189.5 1.1 broadcast.937
  190.5 15.1 %collective-permute-done.18.refs_3_ = bf16[160,512]{1,0:T(8,128)(2,1)S(1)} collective-permute-done((bf16[160,512]{1,0:T(8,128)(2,1)S(1)}, bf16[160,512]{1,0:T(8,128)(2,1)S(1)}, u32[]{:S(2)}, u32[]{:S(2)}) %collective-permute-start.18) | collective-permute-done | bytes 163872 | tf_op jit(solution)/shard_map/ppermute | solution.py:415
  205.7 3.5 %collective-permute-done.19.refs_4_ = bf16[160,512]{1,0:T(8,128)(2,1)S(1)} collective-permute-done((bf16[160,512]{1,0:T(8,128)(2,1)S(1)}, bf16[160,512]{1,0:T(8,128)(2,1)S(1)}, u32[]{:S(2)}, u32[]{:S(2)}) %collective-permute-start.19) | collective-permute-done | bytes 163872 | tf_op jit(solution)/shard_map/ppermute | solution.py:415
  209.2 2.5 collective-permute-done.21.refs_6_
  211.7 2.5 collective-permute-done.22.refs_7_
  214.2 4.0 %shard_map.78 = (bf16[2,128,512]{2,1,0:T(8,128)(2,1)S(1)}, bf16[2,128,512]{2,1,0:T(8,128)(2,1)S(1)}, bf16[2,128,512]{2,1,0:T(8,128)(2,1)S(1)}, bf16[2,128,512]{2,1,0:T(8,128)(2,1)S(1)}) custom-call(s32[8]{0:T(128)S(1)} %get-tuple-element.174.kind_ref, s32[8]{0:T(128)S(1)} %get-tuple-element.173.source_ref, bf16[160,512]{1,0:T(8,128)(2,1)S(1)} %get-tuple-element.146.refs_0_, ...), custom_call_target="tpu_custom_call" | custom-call | tf_op jit(solution)/shard_map/pallas_call | solution.py:341
  218.2 1.0 collective-permute-start.23
  219.3 0.9 collective-permute-start.24
  220.1 4.7 %collective-permute-done.23.refs_3_ = bf16[2,128,512]{2,1,0:T(8,128)(2,1)S(1)} collective-permute-done((bf16[2,128,512]{2,1,0:T(8,128)(2,1)S(1)}, bf16[2,128,512]{2,1,0:T(8,128)(2,1)S(1)}, u32[]{:S(2)}, u32[]{:S(2)}) %collective-permute-start.23) | collective-permute-done | bytes 262176 | tf_op jit(solution)/shard_map/ppermute | solution.py:415
  224.8 6.9 %collective-permute-done.24.refs_4_ = bf16[2,128,512]{2,1,0:T(8,128)(2,1)S(1)} collective-permute-done((bf16[2,128,512]{2,1,0:T(8,128)(2,1)S(1)}, bf16[2,128,512]{2,1,0:T(8,128)(2,1)S(1)}, u32[]{:S(2)}, u32[]{:S(2)}) %collective-permute-start.24) | collective-permute-done | bytes 262176 | tf_op jit(solution)/shard_map/ppermute | solution.py:415
  231.7 0.6 collective-permute-done.25.refs_5_
  232.3 1.9 copy-done.1
  234.2 85.0 %shard_map.79 = bf16[8,128,512]{2,1,0:T(8,128)(2,1)} custom-call(s32[8]{0:T(128)S(1)} %get-tuple-element.172.order_ref, s32[8]{0:T(128)S(1)} %get-tuple-element.206.pick_ref.refs_0_, s32[4]{0:T(128)S(1)} %get-tuple-element.204.spare_ref.refs_1_, bf16[2,128,512]{2,1,0:T(8,128)(2,1)S(1)} %get-tuple-element.157.refs_2_, ...), custom_call_target="tpu_custom_call" | custom-call | flops 23622320128 | bytes 8388608 | tf_op jit(solution)/shard_map/pallas_call | solution.py:370
  (88 shorter events, 3.0 us)
Async XLA Ops:
  1.3 16.3 %all-to-all-start.2 = ((s32[32,2,2,8]{3,1,2,0:T(2,128)}), s32[32,2,2,8]{3,1,2,0:T(2,128)S(1)}, u32[]{:S(2)}, u32[]{:S(2)}) async-start(s32[32,2,2,8]{3,1,2,0:T(2,128)} %broadcast_in_dim.235), calls=%async_computation.2 | async-start | bytes 131072 | tf_op jit(solution)/shard_map/all_to_all | solution.py:443
  9.9 1.2 copy-start
  13.9 7.4 %collective-permute-start = (bf16[48,512]{1,0:T(8,128)(2,1)S(1)}, bf16[48,512]{1,0:T(8,128)(2,1)S(1)}, u32[]{:S(2)}, u32[]{:S(2)}) collective-permute-start(bf16[48,512]{1,0:T(8,128)(2,1)S(1)} %get-tuple-element.108), channel_id=1, source_target_pairs={{0,8},{4,12},{8,16},{12,20},{16,24},{20,28},{24,0},{28,4},{1,9},{5... | collective-permute-start | bytes 147464 | tf_op jit(solution)/shard_map/ppermute | solution.py:415
  15.1 6.2 %collective-permute-start.1 = (bf16[48,512]{1,0:T(8,128)(2,1)S(1)}, bf16[48,512]{1,0:T(8,128)(2,1)S(1)}, u32[]{:S(2)}, u32[]{:S(2)}) collective-permute-start(bf16[48,512]{1,0:T(8,128)(2,1)S(1)} %get-tuple-element.109), channel_id=1, source_target_pairs={{0,16},{4,20},{8,24},{12,28},{16,0},{20,4},{24,8},{28,12},{1,17},{... | collective-permute-start | bytes 147464 | tf_op jit(solution)/shard_map/ppermute | solution.py:415
  16.3 5.2 %collective-permute-start.2 = (bf16[48,512]{1,0:T(8,128)(2,1)S(1)}, bf16[48,512]{1,0:T(8,128)(2,1)S(1)}, u32[]{:S(2)}, u32[]{:S(2)}) collective-permute-start(bf16[48,512]{1,0:T(8,128)(2,1)S(1)} %get-tuple-element.110), channel_id=1, source_target_pairs={{0,24},{4,28},{8,0},{12,4},{16,8},{20,12},{24,16},{28,20},{1,25},{... | collective-permute-start | bytes 147464 | tf_op jit(solution)/shard_map/ppermute | solution.py:415
  22.8 6.2 %collective-permute-start.3 = (bf16[160,512]{1,0:T(8,128)(2,1)S(1)}, bf16[160,512]{1,0:T(8,128)(2,1)S(1)}, u32[]{:S(2)}, u32[]{:S(2)}) collective-permute-start(bf16[160,512]{1,0:T(8,128)(2,1)S(1)} %get-tuple-element.121), channel_id=1, source_target_pairs={{0,4},{4,8},{8,12},{12,16},{16,20},{20,24},{24,28},{28,0},{1,5},{5... | collective-permute-start | bytes 491528 | tf_op jit(solution)/shard_map/ppermute | solution.py:415
  22.9 8.2 %collective-permute-start.4 = (bf16[160,512]{1,0:T(8,128)(2,1)S(1)}, bf16[160,512]{1,0:T(8,128)(2,1)S(1)}, u32[]{:S(2)}, u32[]{:S(2)}) collective-permute-start(bf16[160,512]{1,0:T(8,128)(2,1)S(1)} %get-tuple-element.123), channel_id=1, source_target_pairs={{0,8},{4,12},{8,16},{12,20},{16,24},{20,28},{24,0},{28,4},{1,9},{5... | collective-permute-start | bytes 491528 | tf_op jit(solution)/shard_map/ppermute | solution.py:415
  24.7 21.7 %collective-permute-start.5 = (bf16[160,512]{1,0:T(8,128)(2,1)S(1)}, bf16[160,512]{1,0:T(8,128)(2,1)S(1)}, u32[]{:S(2)}, u32[]{:S(2)}) collective-permute-start(bf16[160,512]{1,0:T(8,128)(2,1)S(1)} %get-tuple-element.124), channel_id=1, source_target_pairs={{0,12},{4,16},{8,20},{12,24},{16,28},{20,0},{24,4},{28,8},{1,13},{... | collective-permute-start | bytes 491528 | tf_op jit(solution)/shard_map/ppermute | solution.py:415
  27.5 22.4 %collective-permute-start.6 = (bf16[160,512]{1,0:T(8,128)(2,1)S(1)}, bf16[160,512]{1,0:T(8,128)(2,1)S(1)}, u32[]{:S(2)}, u32[]{:S(2)}) collective-permute-start(bf16[160,512]{1,0:T(8,128)(2,1)S(1)} %get-tuple-element.125), channel_id=1, source_target_pairs={{0,16},{4,20},{8,24},{12,28},{16,0},{20,4},{24,8},{28,12},{1,17},{... | collective-permute-start | bytes 491528 | tf_op jit(solution)/shard_map/ppermute | solution.py:415
  27.5 22.4 %collective-permute-start.7 = (bf16[160,512]{1,0:T(8,128)(2,1)S(1)}, bf16[160,512]{1,0:T(8,128)(2,1)S(1)}, u32[]{:S(2)}, u32[]{:S(2)}) collective-permute-start(bf16[160,512]{1,0:T(8,128)(2,1)S(1)} %get-tuple-element.126), channel_id=1, source_target_pairs={{0,20},{4,24},{8,28},{12,0},{16,4},{20,8},{24,12},{28,16},{1,21},{... | collective-permute-start | bytes 491528 | tf_op jit(solution)/shard_map/ppermute | solution.py:415
  29.0 26.3 %collective-permute-start.8 = (bf16[160,512]{1,0:T(8,128)(2,1)S(1)}, bf16[160,512]{1,0:T(8,128)(2,1)S(1)}, u32[]{:S(2)}, u32[]{:S(2)}) collective-permute-start(bf16[160,512]{1,0:T(8,128)(2,1)S(1)} %get-tuple-element.127), channel_id=1, source_target_pairs={{0,24},{4,28},{8,0},{12,4},{16,8},{20,12},{24,16},{28,20},{1,25},{... | collective-permute-start | bytes 491528 | tf_op jit(solution)/shard_map/ppermute | solution.py:415
  31.1 25.3 %collective-permute-start.9 = (bf16[160,512]{1,0:T(8,128)(2,1)S(1)}, bf16[160,512]{1,0:T(8,128)(2,1)S(1)}, u32[]{:S(2)}, u32[]{:S(2)}) collective-permute-start(bf16[160,512]{1,0:T(8,128)(2,1)S(1)} %get-tuple-element.128), channel_id=1, source_target_pairs={{0,28},{4,0},{8,4},{12,8},{16,12},{20,16},{24,20},{28,24},{1,29},{... | collective-permute-start | bytes 491528 | tf_op jit(solution)/shard_map/ppermute | solution.py:415
  31.7 42.8 %copy-start.2 = (bf16[2,512,512]{2,1,0:T(8,128)(2,1)S(1)}, bf16[2,512,512]{2,1,0:T(8,128)(2,1)}, u32[]{:S(2)}) copy-start(bf16[2,512,512]{2,1,0:T(8,128)(2,1)} %refs_8_.3) | copy-start | bytes 3145732
  31.7 42.8 %copy-start.3 = (f32[2,2,512]{2,1,0:T(2,128)S(1)}, f32[2,2,512]{2,1,0:T(2,128)}, u32[]{:S(2)}) copy-start(f32[2,2,512]{2,1,0:T(2,128)} %refs_6_.3) | copy-start | bytes 24580
  60.4 7.1 %collective-permute-start.10 = (bf16[2,128,512]{2,1,0:T(8,128)(2,1)S(1)}, bf16[2,128,512]{2,1,0:T(8,128)(2,1)S(1)}, u32[]{:S(2)}, u32[]{:S(2)}) collective-permute-start(bf16[2,128,512]{2,1,0:T(8,128)(2,1)S(1)} %get-tuple-element.131), channel_id=1, source_target_pairs={{0,1},{1,2},{2,3},{3,0},{4,5},{5,6},{6,7},{7,4},{8,9},{9,10},{10,1... | collective-permute-start | bytes 786440 | tf_op jit(solution)/shard_map/ppermute | solution.py:415
  62.1 11.8 %collective-permute-start.11 = (bf16[2,128,512]{2,1,0:T(8,128)(2,1)S(1)}, bf16[2,128,512]{2,1,0:T(8,128)(2,1)S(1)}, u32[]{:S(2)}, u32[]{:S(2)}) collective-permute-start(bf16[2,128,512]{2,1,0:T(8,128)(2,1)S(1)} %get-tuple-element.132), channel_id=1, source_target_pairs={{0,2},{1,3},{2,0},{3,1},{4,6},{5,7},{6,4},{7,5},{8,10},{9,11},{10,... | collective-permute-start | bytes 786440 | tf_op jit(solution)/shard_map/ppermute | solution.py:415
  62.3 12.2 %collective-permute-start.12 = (bf16[2,128,512]{2,1,0:T(8,128)(2,1)S(1)}, bf16[2,128,512]{2,1,0:T(8,128)(2,1)S(1)}, u32[]{:S(2)}, u32[]{:S(2)}) collective-permute-start(bf16[2,128,512]{2,1,0:T(8,128)(2,1)S(1)} %get-tuple-element.133), channel_id=1, source_target_pairs={{0,3},{1,0},{2,1},{3,2},{4,7},{5,4},{6,5},{7,6},{8,11},{9,8},{10,9... | collective-permute-start | bytes 786440 | tf_op jit(solution)/shard_map/ppermute | solution.py:415
  174.0 3.3 %collective-permute-start.13 = (bf16[32,512]{1,0:T(8,128)(2,1)S(1)}, bf16[32,512]{1,0:T(8,128)(2,1)S(1)}, u32[]{:S(2)}, u32[]{:S(2)}) collective-permute-start(bf16[32,512]{1,0:T(8,128)(2,1)S(1)} %get-tuple-element.135), channel_id=1, source_target_pairs={{0,8},{4,12},{8,16},{12,20},{16,24},{20,28},{24,0},{28,4},{1,9},{5... | collective-permute-start | bytes 98312 | tf_op jit(solution)/shard_map/ppermute | solution.py:415
  174.1 4.2 %collective-permute-start.14 = (bf16[32,512]{1,0:T(8,128)(2,1)S(1)}, bf16[32,512]{1,0:T(8,128)(2,1)S(1)}, u32[]{:S(2)}, u32[]{:S(2)}) collective-permute-start(bf16[32,512]{1,0:T(8,128)(2,1)S(1)} %get-tuple-element.136), channel_id=1, source_target_pairs={{0,16},{4,20},{8,24},{12,28},{16,0},{20,4},{24,8},{28,12},{1,17},{... | collective-permute-start | bytes 98312 | tf_op jit(solution)/shard_map/ppermute | solution.py:415
  174.2 5.7 %collective-permute-start.15 = (bf16[32,512]{1,0:T(8,128)(2,1)S(1)}, bf16[32,512]{1,0:T(8,128)(2,1)S(1)}, u32[]{:S(2)}, u32[]{:S(2)}) collective-permute-start(bf16[32,512]{1,0:T(8,128)(2,1)S(1)} %get-tuple-element.137), channel_id=1, source_target_pairs={{0,24},{4,28},{8,0},{12,4},{16,8},{20,12},{24,16},{28,20},{1,25},{... | collective-permute-start | bytes 98312 | tf_op jit(solution)/shard_map/ppermute | solution.py:415
  181.1 5.4 %collective-permute-start.16 = (bf16[160,512]{1,0:T(8,128)(2,1)S(1)}, bf16[160,512]{1,0:T(8,128)(2,1)S(1)}, u32[]{:S(2)}, u32[]{:S(2)}) collective-permute-start(bf16[160,512]{1,0:T(8,128)(2,1)S(1)} %get-tuple-element.148), channel_id=1, source_target_pairs={{0,4},{4,8},{8,12},{12,16},{16,20},{20,24},{24,28},{28,0},{1,5},{5... | collective-permute-start | bytes 491528 | tf_op jit(solution)/shard_map/ppermute | solution.py:415
  181.2 8.1 %collective-permute-start.17 = (bf16[160,512]{1,0:T(8,128)(2,1)S(1)}, bf16[160,512]{1,0:T(8,128)(2,1)S(1)}, u32[]{:S(2)}, u32[]{:S(2)}) collective-permute-start(bf16[160,512]{1,0:T(8,128)(2,1)S(1)} %get-tuple-element.150), channel_id=1, source_target_pairs={{0,8},{4,12},{8,16},{12,20},{16,24},{20,28},{24,0},{28,4},{1,9},{5... | collective-permute-start | bytes 491528 | tf_op jit(solution)/shard_map/ppermute | solution.py:415
  181.8 23.9 %collective-permute-start.18 = (bf16[160,512]{1,0:T(8,128)(2,1)S(1)}, bf16[160,512]{1,0:T(8,128)(2,1)S(1)}, u32[]{:S(2)}, u32[]{:S(2)}) collective-permute-start(bf16[160,512]{1,0:T(8,128)(2,1)S(1)} %get-tuple-element.151), channel_id=1, source_target_pairs={{0,12},{4,16},{8,20},{12,24},{16,28},{20,0},{24,4},{28,8},{1,13},{... | collective-permute-start | bytes 491528 | tf_op jit(solution)/shard_map/ppermute | solution.py:415
  184.9 24.3 %collective-permute-start.19 = (bf16[160,512]{1,0:T(8,128)(2,1)S(1)}, bf16[160,512]{1,0:T(8,128)(2,1)S(1)}, u32[]{:S(2)}, u32[]{:S(2)}) collective-permute-start(bf16[160,512]{1,0:T(8,128)(2,1)S(1)} %get-tuple-element.152), channel_id=1, source_target_pairs={{0,16},{4,20},{8,24},{12,28},{16,0},{20,4},{24,8},{28,12},{1,17},{... | collective-permute-start | bytes 491528 | tf_op jit(solution)/shard_map/ppermute | solution.py:415
  184.9 24.3 %collective-permute-start.20 = (bf16[160,512]{1,0:T(8,128)(2,1)S(1)}, bf16[160,512]{1,0:T(8,128)(2,1)S(1)}, u32[]{:S(2)}, u32[]{:S(2)}) collective-permute-start(bf16[160,512]{1,0:T(8,128)(2,1)S(1)} %get-tuple-element.153), channel_id=1, source_target_pairs={{0,20},{4,24},{8,28},{12,0},{16,4},{20,8},{24,12},{28,16},{1,21},{... | collective-permute-start | bytes 491528 | tf_op jit(solution)/shard_map/ppermute | solution.py:415
  186.5 25.2 %collective-permute-start.21 = (bf16[160,512]{1,0:T(8,128)(2,1)S(1)}, bf16[160,512]{1,0:T(8,128)(2,1)S(1)}, u32[]{:S(2)}, u32[]{:S(2)}) collective-permute-start(bf16[160,512]{1,0:T(8,128)(2,1)S(1)} %get-tuple-element.154), channel_id=1, source_target_pairs={{0,24},{4,28},{8,0},{12,4},{16,8},{20,12},{24,16},{28,20},{1,25},{... | collective-permute-start | bytes 491528 | tf_op jit(solution)/shard_map/ppermute | solution.py:415
  189.3 24.9 %collective-permute-start.22 = (bf16[160,512]{1,0:T(8,128)(2,1)S(1)}, bf16[160,512]{1,0:T(8,128)(2,1)S(1)}, u32[]{:S(2)}, u32[]{:S(2)}) collective-permute-start(bf16[160,512]{1,0:T(8,128)(2,1)S(1)} %get-tuple-element.155), channel_id=1, source_target_pairs={{0,28},{4,0},{8,4},{12,8},{16,12},{20,16},{24,20},{28,24},{1,29},{... | collective-permute-start | bytes 491528 | tf_op jit(solution)/shard_map/ppermute | solution.py:415
  218.2 6.6 %collective-permute-start.23 = (bf16[2,128,512]{2,1,0:T(8,128)(2,1)S(1)}, bf16[2,128,512]{2,1,0:T(8,128)(2,1)S(1)}, u32[]{:S(2)}, u32[]{:S(2)}) collective-permute-start(bf16[2,128,512]{2,1,0:T(8,128)(2,1)S(1)} %get-tuple-element.158), channel_id=1, source_target_pairs={{0,1},{1,2},{2,3},{3,0},{4,5},{5,6},{6,7},{7,4},{8,9},{9,10},{10,1... | collective-permute-start | bytes 786440 | tf_op jit(solution)/shard_map/ppermute | solution.py:415
  219.3 12.4 %collective-permute-start.24 = (bf16[2,128,512]{2,1,0:T(8,128)(2,1)S(1)}, bf16[2,128,512]{2,1,0:T(8,128)(2,1)S(1)}, u32[]{:S(2)}, u32[]{:S(2)}) collective-permute-start(bf16[2,128,512]{2,1,0:T(8,128)(2,1)S(1)} %get-tuple-element.159), channel_id=1, source_target_pairs={{0,2},{1,3},{2,0},{3,1},{4,6},{5,7},{6,4},{7,5},{8,10},{9,11},{10,... | collective-permute-start | bytes 786440 | tf_op jit(solution)/shard_map/ppermute | solution.py:415
  220.1 12.2 %collective-permute-start.25 = (bf16[2,128,512]{2,1,0:T(8,128)(2,1)S(1)}, bf16[2,128,512]{2,1,0:T(8,128)(2,1)S(1)}, u32[]{:S(2)}, u32[]{:S(2)}) collective-permute-start(bf16[2,128,512]{2,1,0:T(8,128)(2,1)S(1)} %get-tuple-element.160), channel_id=1, source_target_pairs={{0,3},{1,0},{2,1},{3,2},{4,7},{5,4},{6,5},{7,6},{8,11},{9,8},{10,9... | collective-permute-start | bytes 786440 | tf_op jit(solution)/shard_map/ppermute | solution.py:415
  232.3 1.9 copy-start.1

commit v4 on v3

--- a/solution.py
+++ b/solution.py
@@ -264,12 +264,12 @@
     for tile in range(width // LANES):
         v_ref[tile, :, :LANES] = values[:, tile * LANES : (tile + 1) * LANES]
 
-    arrive(1)
-    arrive(2)
-    arrive(3)
-
     def finish(shifted):
         safe = attend(q_ref, k_ref, v_ref, mixed_ref, shifted)
+        if not shifted:
+            arrive(1)
+            arrive(2)
+            arrive(3)
         mixed = (x.astype(F32) + matmul(mixed_ref[...], wout_ref[...])).astype(BF16)
         inner = normalize(mixed.astype(F32), gain_ref[layer, 1:2, :]).astype(BF16)
         total = mixed.astype(F32)

time: 318 us -> 316 us (level)
  no operation moved by 1% of the time
where the time goes in v4:
time: 316 us; the launch traced here: 319 us
  Pallas kernels  197 us (62%)
  waiting for transfers between devices  77.9 us (25%)
  starting transfers between devices  29.4 us (9%)
  local copies, waits for them, and re-layouts  8.5 us (3%)
  other arithmetic  3.59 us (1%)
    pallas_call x2, Pallas kernels, encoder_layer(): pl.pallas_call(functools.partial(layer_kernel, layer, columns, peers), gr...  184 us
    ppermute x26, waiting for transfers between devices, shifted(): lax.ppermute(arrays[d], axis, [(i, (i + d * step) % size) for i in range(...  77.9 us
    ppermute x26, starting transfers between devices, shifted(): lax.ppermute(arrays[d], axis, [(i, (i + d * step) % size) for i in range(...  23.1 us
    pallas_call x2, Pallas kernels, turn_bricks(): pl.pallas_call(functools.partial(turn_kernel, peers), in_specs=[SMEM] * 2...  8.1 us
  transfers between devices with their start and end apart: 27, of which 20 were waited for; matrix products, arithmetic and copies ran while one was open for 2% of the time, Pallas kernels for 1%

profile of v4, /device:TPU:13, one launch (start us, length us, event | category | flops | bytes accessed | tf_op | source)
XLA Modules:
  0.0 318.5 jit_solution(17553358817092203536)
XLA Ops:
  0.0 0.7 copy.48
  0.7 0.6 broadcast_in_dim.235
  1.3 6.3 %all-to-all-start.2 = ((s32[32,2,2,8]{3,1,2,0:T(2,128)}), s32[32,2,2,8]{3,1,2,0:T(2,128)S(1)}, u32[]{:S(2)}, u32[]{:S(2)}) async-start(s32[32,2,2,8]{3,1,2,0:T(2,128)} %broadcast_in_dim.235), calls=%async_computation.2 | async-start | bytes 131072 | tf_op jit(solution)/shard_map/all_to_all | solution.py:443
  7.7 0.2 convert_reduce_fusion.3
  8.0 0.2 reduce_window_sum.22
  8.2 0.7 fusion.40
  8.9 0.1 select_reduce_fusion.10
  9.0 0.2 select_reduce_fusion.4
  9.9 1.2 copy-done
  11.2 2.7 shard_map.73
  13.9 1.3 collective-permute-start
  15.1 1.2 collective-permute-start.1
  16.3 1.3 collective-permute-start.2
  18.4 0.2 convert_reduce_fusion
  18.6 0.6 reduce_max.9
  21.5 1.4 shard_map.74
  22.9 1.5 collective-permute-start.4
  24.4 0.2 fusion.9
  24.7 2.8 collective-permute-start.5
  27.5 1.5 collective-permute-start.7
  29.0 2.0 collective-permute-start.8
  31.1 0.3 collective-permute-start.9
  31.4 0.1 select_reduce_fusion.6
  31.7 1.1 conditional.2
  31.8 1.1 broadcast.928
  32.8 13.6 %collective-permute-done.5.refs_3_ = bf16[160,512]{1,0:T(8,128)(2,1)S(1)} collective-permute-done((bf16[160,512]{1,0:T(8,128)(2,1)S(1)}, bf16[160,512]{1,0:T(8,128)(2,1)S(1)}, u32[]{:S(2)}, u32[]{:S(2)}) %collective-permute-start.5) | collective-permute-done | bytes 163872 | tf_op jit(solution)/shard_map/ppermute | solution.py:415
  46.4 3.5 %collective-permute-done.6.refs_4_ = bf16[160,512]{1,0:T(8,128)(2,1)S(1)} collective-permute-done((bf16[160,512]{1,0:T(8,128)(2,1)S(1)}, bf16[160,512]{1,0:T(8,128)(2,1)S(1)}, u32[]{:S(2)}, u32[]{:S(2)}) %collective-permute-start.6) | collective-permute-done | bytes 163872 | tf_op jit(solution)/shard_map/ppermute | solution.py:415
  50.0 5.3 %collective-permute-done.8.refs_6_ = bf16[160,512]{1,0:T(8,128)(2,1)S(1)} collective-permute-done((bf16[160,512]{1,0:T(8,128)(2,1)S(1)}, bf16[160,512]{1,0:T(8,128)(2,1)S(1)}, u32[]{:S(2)}, u32[]{:S(2)}) %collective-permute-start.8) | collective-permute-done | bytes 163872 | tf_op jit(solution)/shard_map/ppermute | solution.py:415
  55.3 1.1 collective-permute-done.9.refs_7_
  56.4 4.0 %shard_map.75 = (bf16[2,128,512]{2,1,0:T(8,128)(2,1)S(1)}, bf16[2,128,512]{2,1,0:T(8,128)(2,1)S(1)}, bf16[2,128,512]{2,1,0:T(8,128)(2,1)S(1)}, bf16[2,128,512]{2,1,0:T(8,128)(2,1)S(1)}) custom-call(s32[8]{0:T(128)S(1)} %get-tuple-element.170.kind_ref, s32[8]{0:T(128)S(1)} %get-tuple-element.169.source_ref, bf16[160,512]{1,0:T(8,128)(2,1)S(1)} %get-tuple-element.119.refs_0_, ...), custom_call_target="tpu_custom_call" | custom-call | tf_op jit(solution)/shard_map/pallas_call | solution.py:341
  60.4 1.6 collective-permute-start.10
  62.1 0.3 collective-permute-start.11
  62.3 0.2 collective-permute-start.12
  62.7 4.9 %collective-permute-done.10.refs_3_ = bf16[2,128,512]{2,1,0:T(8,128)(2,1)S(1)} collective-permute-done((bf16[2,128,512]{2,1,0:T(8,128)(2,1)S(1)}, bf16[2,128,512]{2,1,0:T(8,128)(2,1)S(1)}, u32[]{:S(2)}, u32[]{:S(2)}) %collective-permute-start.10) | collective-permute-done | bytes 262176 | tf_op jit(solution)/shard_map/ppermute | solution.py:415
  67.6 6.3 %collective-permute-done.11.refs_4_ = bf16[2,128,512]{2,1,0:T(8,128)(2,1)S(1)} collective-permute-done((bf16[2,128,512]{2,1,0:T(8,128)(2,1)S(1)}, bf16[2,128,512]{2,1,0:T(8,128)(2,1)S(1)}, u32[]{:S(2)}, u32[]{:S(2)}) %collective-permute-start.11) | collective-permute-done | bytes 262176 | tf_op jit(solution)/shard_map/ppermute | solution.py:415
  73.9 0.6 collective-permute-done.12.refs_5_
  74.5 99.4 %shard_map.76 = (bf16[160,512]{1,0:T(8,128)(2,1)S(1)}, bf16[160,512]{1,0:T(8,128)(2,1)S(1)}, bf16[160,512]{1,0:T(8,128)(2,1)S(1)}, bf16[160,512]{1,0:T(8,128)(2,...) custom-call(s32[8]{0:T(128)S(1)} %get-tuple-element.171.order_ref, ...), custom_call_target="tpu_custom_call" | custom-call | flops 23622320128 | bytes 8388608 | tf_op jit(solution)/shard_map/pallas_call | solution.py:370
  174.1 1.4 collective-permute-start.15
  175.5 0.2 select_reduce_fusion.11.goal_ref
  175.6 1.6 collective-permute-done.13.refs_1_
  177.2 1.0 collective-permute-done.14.refs_2_
  178.2 1.6 collective-permute-done.15.refs_3_
  179.7 1.2 shard_map.77
  181.0 0.7 collective-permute-start.17
  181.8 3.0 collective-permute-start.18
  184.8 1.2 collective-permute-start.20
  186.0 0.3 collective-permute-done.16.refs_1_
  186.4 0.7 collective-permute-start.21
  187.1 2.1 collective-permute-done.17.refs_2_
  189.2 0.1 select_reduce_fusion.8
  189.3 1.1 conditional.3
  189.3 1.1 broadcast.937
  190.4 15.1 %collective-permute-done.18.refs_3_ = bf16[160,512]{1,0:T(8,128)(2,1)S(1)} collective-permute-done((bf16[160,512]{1,0:T(8,128)(2,1)S(1)}, bf16[160,512]{1,0:T(8,128)(2,1)S(1)}, u32[]{:S(2)}, u32[]{:S(2)}) %collective-permute-start.18) | collective-permute-done | bytes 163872 | tf_op jit(solution)/shard_map/ppermute | solution.py:415
  205.5 3.5 %collective-permute-done.19.refs_4_ = bf16[160,512]{1,0:T(8,128)(2,1)S(1)} collective-permute-done((bf16[160,512]{1,0:T(8,128)(2,1)S(1)}, bf16[160,512]{1,0:T(8,128)(2,1)S(1)}, u32[]{:S(2)}, u32[]{:S(2)}) %collective-permute-start.19) | collective-permute-done | bytes 163872 | tf_op jit(solution)/shard_map/ppermute | solution.py:415
  209.1 2.5 collective-permute-done.21.refs_6_
  211.5 2.5 collective-permute-done.22.refs_7_
  214.0 4.0 %shard_map.78 = (bf16[2,128,512]{2,1,0:T(8,128)(2,1)S(1)}, bf16[2,128,512]{2,1,0:T(8,128)(2,1)S(1)}, bf16[2,128,512]{2,1,0:T(8,128)(2,1)S(1)}, bf16[2,128,512]{2,1,0:T(8,128)(2,1)S(1)}) custom-call(s32[8]{0:T(128)S(1)} %get-tuple-element.174.kind_ref, s32[8]{0:T(128)S(1)} %get-tuple-element.173.source_ref, bf16[160,512]{1,0:T(8,128)(2,1)S(1)} %get-tuple-element.146.refs_0_, ...), custom_call_target="tpu_custom_call" | custom-call | tf_op jit(solution)/shard_map/pallas_call | solution.py:341
  218.1 1.1 collective-permute-start.23
  219.2 0.8 collective-permute-start.24
  220.0 4.7 %collective-permute-done.23.refs_3_ = bf16[2,128,512]{2,1,0:T(8,128)(2,1)S(1)} collective-permute-done((bf16[2,128,512]{2,1,0:T(8,128)(2,1)S(1)}, bf16[2,128,512]{2,1,0:T(8,128)(2,1)S(1)}, u32[]{:S(2)}, u32[]{:S(2)}) %collective-permute-start.23) | collective-permute-done | bytes 262176 | tf_op jit(solution)/shard_map/ppermute | solution.py:415
  224.7 6.9 %collective-permute-done.24.refs_4_ = bf16[2,128,512]{2,1,0:T(8,128)(2,1)S(1)} collective-permute-done((bf16[2,128,512]{2,1,0:T(8,128)(2,1)S(1)}, bf16[2,128,512]{2,1,0:T(8,128)(2,1)S(1)}, u32[]{:S(2)}, u32[]{:S(2)}) %collective-permute-start.24) | collective-permute-done | bytes 262176 | tf_op jit(solution)/shard_map/ppermute | solution.py:415
  231.6 0.6 collective-permute-done.25.refs_5_
  232.2 1.9 copy-done.1
  234.1 84.2 %shard_map.79 = bf16[8,128,512]{2,1,0:T(8,128)(2,1)} custom-call(s32[8]{0:T(128)S(1)} %get-tuple-element.172.order_ref, s32[8]{0:T(128)S(1)} %get-tuple-element.206.pick_ref.refs_0_, s32[4]{0:T(128)S(1)} %get-tuple-element.204.spare_ref.refs_1_, bf16[2,128,512]{2,1,0:T(8,128)(2,1)S(1)} %get-tuple-element.157.refs_2_, ...), custom_call_target="tpu_custom_call" | custom-call | flops 23622320128 | bytes 8388608 | tf_op jit(solution)/shard_map/pallas_call | solution.py:370
  (88 shorter events, 3.0 us)
Async XLA Ops:
  1.3 16.3 %all-to-all-start.2 = ((s32[32,2,2,8]{3,1,2,0:T(2,128)}), s32[32,2,2,8]{3,1,2,0:T(2,128)S(1)}, u32[]{:S(2)}, u32[]{:S(2)}) async-start(s32[32,2,2,8]{3,1,2,0:T(2,128)} %broadcast_in_dim.235), calls=%async_computation.2 | async-start | bytes 131072 | tf_op jit(solution)/shard_map/all_to_all | solution.py:443
  9.9 1.2 copy-start
  13.9 7.4 %collective-permute-start = (bf16[48,512]{1,0:T(8,128)(2,1)S(1)}, bf16[48,512]{1,0:T(8,128)(2,1)S(1)}, u32[]{:S(2)}, u32[]{:S(2)}) collective-permute-start(bf16[48,512]{1,0:T(8,128)(2,1)S(1)} %get-tuple-element.108), channel_id=1, source_target_pairs={{0,8},{4,12},{8,16},{12,20},{16,24},{20,28},{24,0},{28,4},{1,9},{5... | collective-permute-start | bytes 147464 | tf_op jit(solution)/shard_map/ppermute | solution.py:415
  15.1 6.2 %collective-permute-start.1 = (bf16[48,512]{1,0:T(8,128)(2,1)S(1)}, bf16[48,512]{1,0:T(8,128)(2,1)S(1)}, u32[]{:S(2)}, u32[]{:S(2)}) collective-permute-start(bf16[48,512]{1,0:T(8,128)(2,1)S(1)} %get-tuple-element.109), channel_id=1, source_target_pairs={{0,16},{4,20},{8,24},{12,28},{16,0},{20,4},{24,8},{28,12},{1,17},{... | collective-permute-start | bytes 147464 | tf_op jit(solution)/shard_map/ppermute | solution.py:415
  16.3 5.2 %collective-permute-start.2 = (bf16[48,512]{1,0:T(8,128)(2,1)S(1)}, bf16[48,512]{1,0:T(8,128)(2,1)S(1)}, u32[]{:S(2)}, u32[]{:S(2)}) collective-permute-start(bf16[48,512]{1,0:T(8,128)(2,1)S(1)} %get-tuple-element.110), channel_id=1, source_target_pairs={{0,24},{4,28},{8,0},{12,4},{16,8},{20,12},{24,16},{28,20},{1,25},{... | collective-permute-start | bytes 147464 | tf_op jit(solution)/shard_map/ppermute | solution.py:415
  22.8 6.2 %collective-permute-start.3 = (bf16[160,512]{1,0:T(8,128)(2,1)S(1)}, bf16[160,512]{1,0:T(8,128)(2,1)S(1)}, u32[]{:S(2)}, u32[]{:S(2)}) collective-permute-start(bf16[160,512]{1,0:T(8,128)(2,1)S(1)} %get-tuple-element.121), channel_id=1, source_target_pairs={{0,4},{4,8},{8,12},{12,16},{16,20},{20,24},{24,28},{28,0},{1,5},{5... | collective-permute-start | bytes 491528 | tf_op jit(solution)/shard_map/ppermute | solution.py:415
  22.9 8.2 %collective-permute-start.4 = (bf16[160,512]{1,0:T(8,128)(2,1)S(1)}, bf16[160,512]{1,0:T(8,128)(2,1)S(1)}, u32[]{:S(2)}, u32[]{:S(2)}) collective-permute-start(bf16[160,512]{1,0:T(8,128)(2,1)S(1)} %get-tuple-element.123), channel_id=1, source_target_pairs={{0,8},{4,12},{8,16},{12,20},{16,24},{20,28},{24,0},{28,4},{1,9},{5... | collective-permute-start | bytes 491528 | tf_op jit(solution)/shard_map/ppermute | solution.py:415
  24.7 21.7 %collective-permute-start.5 = (bf16[160,512]{1,0:T(8,128)(2,1)S(1)}, bf16[160,512]{1,0:T(8,128)(2,1)S(1)}, u32[]{:S(2)}, u32[]{:S(2)}) collective-permute-start(bf16[160,512]{1,0:T(8,128)(2,1)S(1)} %get-tuple-element.124), channel_id=1, source_target_pairs={{0,12},{4,16},{8,20},{12,24},{16,28},{20,0},{24,4},{28,8},{1,13},{... | collective-permute-start | bytes 491528 | tf_op jit(solution)/shard_map/ppermute | solution.py:415
  27.5 22.4 %collective-permute-start.6 = (bf16[160,512]{1,0:T(8,128)(2,1)S(1)}, bf16[160,512]{1,0:T(8,128)(2,1)S(1)}, u32[]{:S(2)}, u32[]{:S(2)}) collective-permute-start(bf16[160,512]{1,0:T(8,128)(2,1)S(1)} %get-tuple-element.125), channel_id=1, source_target_pairs={{0,16},{4,20},{8,24},{12,28},{16,0},{20,4},{24,8},{28,12},{1,17},{... | collective-permute-start | bytes 491528 | tf_op jit(solution)/shard_map/ppermute | solution.py:415
  27.5 22.4 %collective-permute-start.7 = (bf16[160,512]{1,0:T(8,128)(2,1)S(1)}, bf16[160,512]{1,0:T(8,128)(2,1)S(1)}, u32[]{:S(2)}, u32[]{:S(2)}) collective-permute-start(bf16[160,512]{1,0:T(8,128)(2,1)S(1)} %get-tuple-element.126), channel_id=1, source_target_pairs={{0,20},{4,24},{8,28},{12,0},{16,4},{20,8},{24,12},{28,16},{1,21},{... | collective-permute-start | bytes 491528 | tf_op jit(solution)/shard_map/ppermute | solution.py:415
  29.0 26.3 %collective-permute-start.8 = (bf16[160,512]{1,0:T(8,128)(2,1)S(1)}, bf16[160,512]{1,0:T(8,128)(2,1)S(1)}, u32[]{:S(2)}, u32[]{:S(2)}) collective-permute-start(bf16[160,512]{1,0:T(8,128)(2,1)S(1)} %get-tuple-element.127), channel_id=1, source_target_pairs={{0,24},{4,28},{8,0},{12,4},{16,8},{20,12},{24,16},{28,20},{1,25},{... | collective-permute-start | bytes 491528 | tf_op jit(solution)/shard_map/ppermute | solution.py:415
  31.1 25.3 %collective-permute-start.9 = (bf16[160,512]{1,0:T(8,128)(2,1)S(1)}, bf16[160,512]{1,0:T(8,128)(2,1)S(1)}, u32[]{:S(2)}, u32[]{:S(2)}) collective-permute-start(bf16[160,512]{1,0:T(8,128)(2,1)S(1)} %get-tuple-element.128), channel_id=1, source_target_pairs={{0,28},{4,0},{8,4},{12,8},{16,12},{20,16},{24,20},{28,24},{1,29},{... | collective-permute-start | bytes 491528 | tf_op jit(solution)/shard_map/ppermute | solution.py:415
  31.7 42.8 %copy-start.2 = (bf16[2,512,512]{2,1,0:T(8,128)(2,1)S(1)}, bf16[2,512,512]{2,1,0:T(8,128)(2,1)}, u32[]{:S(2)}) copy-start(bf16[2,512,512]{2,1,0:T(8,128)(2,1)} %refs_8_.3) | copy-start | bytes 3145732
  31.7 42.8 %copy-start.3 = (f32[2,2,512]{2,1,0:T(2,128)S(1)}, f32[2,2,512]{2,1,0:T(2,128)}, u32[]{:S(2)}) copy-start(f32[2,2,512]{2,1,0:T(2,128)} %refs_6_.3) | copy-start | bytes 24580
  60.4 7.1 %collective-permute-start.10 = (bf16[2,128,512]{2,1,0:T(8,128)(2,1)S(1)}, bf16[2,128,512]{2,1,0:T(8,128)(2,1)S(1)}, u32[]{:S(2)}, u32[]{:S(2)}) collective-permute-start(bf16[2,128,512]{2,1,0:T(8,128)(2,1)S(1)} %get-tuple-element.131), channel_id=1, source_target_pairs={{0,1},{1,2},{2,3},{3,0},{4,5},{5,6},{6,7},{7,4},{8,9},{9,10},{10,1... | collective-permute-start | bytes 786440 | tf_op jit(solution)/shard_map/ppermute | solution.py:415
  62.1 11.8 %collective-permute-start.11 = (bf16[2,128,512]{2,1,0:T(8,128)(2,1)S(1)}, bf16[2,128,512]{2,1,0:T(8,128)(2,1)S(1)}, u32[]{:S(2)}, u32[]{:S(2)}) collective-permute-start(bf16[2,128,512]{2,1,0:T(8,128)(2,1)S(1)} %get-tuple-element.132), channel_id=1, source_target_pairs={{0,2},{1,3},{2,0},{3,1},{4,6},{5,7},{6,4},{7,5},{8,10},{9,11},{10,... | collective-permute-start | bytes 786440 | tf_op jit(solution)/shard_map/ppermute | solution.py:415
  62.3 12.2 %collective-permute-start.12 = (bf16[2,128,512]{2,1,0:T(8,128)(2,1)S(1)}, bf16[2,128,512]{2,1,0:T(8,128)(2,1)S(1)}, u32[]{:S(2)}, u32[]{:S(2)}) collective-permute-start(bf16[2,128,512]{2,1,0:T(8,128)(2,1)S(1)} %get-tuple-element.133), channel_id=1, source_target_pairs={{0,3},{1,0},{2,1},{3,2},{4,7},{5,4},{6,5},{7,6},{8,11},{9,8},{10,9... | collective-permute-start | bytes 786440 | tf_op jit(solution)/shard_map/ppermute | solution.py:415
  173.9 3.3 %collective-permute-start.13 = (bf16[32,512]{1,0:T(8,128)(2,1)S(1)}, bf16[32,512]{1,0:T(8,128)(2,1)S(1)}, u32[]{:S(2)}, u32[]{:S(2)}) collective-permute-start(bf16[32,512]{1,0:T(8,128)(2,1)S(1)} %get-tuple-element.135), channel_id=1, source_target_pairs={{0,8},{4,12},{8,16},{12,20},{16,24},{20,28},{24,0},{28,4},{1,9},{5... | collective-permute-start | bytes 98312 | tf_op jit(solution)/shard_map/ppermute | solution.py:415
  174.0 4.2 %collective-permute-start.14 = (bf16[32,512]{1,0:T(8,128)(2,1)S(1)}, bf16[32,512]{1,0:T(8,128)(2,1)S(1)}, u32[]{:S(2)}, u32[]{:S(2)}) collective-permute-start(bf16[32,512]{1,0:T(8,128)(2,1)S(1)} %get-tuple-element.136), channel_id=1, source_target_pairs={{0,16},{4,20},{8,24},{12,28},{16,0},{20,4},{24,8},{28,12},{1,17},{... | collective-permute-start | bytes 98312 | tf_op jit(solution)/shard_map/ppermute | solution.py:415
  174.1 5.7 %collective-permute-start.15 = (bf16[32,512]{1,0:T(8,128)(2,1)S(1)}, bf16[32,512]{1,0:T(8,128)(2,1)S(1)}, u32[]{:S(2)}, u32[]{:S(2)}) collective-permute-start(bf16[32,512]{1,0:T(8,128)(2,1)S(1)} %get-tuple-element.137), channel_id=1, source_target_pairs={{0,24},{4,28},{8,0},{12,4},{16,8},{20,12},{24,16},{28,20},{1,25},{... | collective-permute-start | bytes 98312 | tf_op jit(solution)/shard_map/ppermute | solution.py:415
  181.0 5.4 %collective-permute-start.16 = (bf16[160,512]{1,0:T(8,128)(2,1)S(1)}, bf16[160,512]{1,0:T(8,128)(2,1)S(1)}, u32[]{:S(2)}, u32[]{:S(2)}) collective-permute-start(bf16[160,512]{1,0:T(8,128)(2,1)S(1)} %get-tuple-element.148), channel_id=1, source_target_pairs={{0,4},{4,8},{8,12},{12,16},{16,20},{20,24},{24,28},{28,0},{1,5},{5... | collective-permute-start | bytes 491528 | tf_op jit(solution)/shard_map/ppermute | solution.py:415
  181.0 8.1 %collective-permute-start.17 = (bf16[160,512]{1,0:T(8,128)(2,1)S(1)}, bf16[160,512]{1,0:T(8,128)(2,1)S(1)}, u32[]{:S(2)}, u32[]{:S(2)}) collective-permute-start(bf16[160,512]{1,0:T(8,128)(2,1)S(1)} %get-tuple-element.150), channel_id=1, source_target_pairs={{0,8},{4,12},{8,16},{12,20},{16,24},{20,28},{24,0},{28,4},{1,9},{5... | collective-permute-start | bytes 491528 | tf_op jit(solution)/shard_map/ppermute | solution.py:415
  181.8 23.8 %collective-permute-start.18 = (bf16[160,512]{1,0:T(8,128)(2,1)S(1)}, bf16[160,512]{1,0:T(8,128)(2,1)S(1)}, u32[]{:S(2)}, u32[]{:S(2)}) collective-permute-start(bf16[160,512]{1,0:T(8,128)(2,1)S(1)} %get-tuple-element.151), channel_id=1, source_target_pairs={{0,12},{4,16},{8,20},{12,24},{16,28},{20,0},{24,4},{28,8},{1,13},{... | collective-permute-start | bytes 491528 | tf_op jit(solution)/shard_map/ppermute | solution.py:415
  184.8 24.3 %collective-permute-start.19 = (bf16[160,512]{1,0:T(8,128)(2,1)S(1)}, bf16[160,512]{1,0:T(8,128)(2,1)S(1)}, u32[]{:S(2)}, u32[]{:S(2)}) collective-permute-start(bf16[160,512]{1,0:T(8,128)(2,1)S(1)} %get-tuple-element.152), channel_id=1, source_target_pairs={{0,16},{4,20},{8,24},{12,28},{16,0},{20,4},{24,8},{28,12},{1,17},{... | collective-permute-start | bytes 491528 | tf_op jit(solution)/shard_map/ppermute | solution.py:415
  184.8 24.3 %collective-permute-start.20 = (bf16[160,512]{1,0:T(8,128)(2,1)S(1)}, bf16[160,512]{1,0:T(8,128)(2,1)S(1)}, u32[]{:S(2)}, u32[]{:S(2)}) collective-permute-start(bf16[160,512]{1,0:T(8,128)(2,1)S(1)} %get-tuple-element.153), channel_id=1, source_target_pairs={{0,20},{4,24},{8,28},{12,0},{16,4},{20,8},{24,12},{28,16},{1,21},{... | collective-permute-start | bytes 491528 | tf_op jit(solution)/shard_map/ppermute | solution.py:415
  186.4 25.2 %collective-permute-start.21 = (bf16[160,512]{1,0:T(8,128)(2,1)S(1)}, bf16[160,512]{1,0:T(8,128)(2,1)S(1)}, u32[]{:S(2)}, u32[]{:S(2)}) collective-permute-start(bf16[160,512]{1,0:T(8,128)(2,1)S(1)} %get-tuple-element.154), channel_id=1, source_target_pairs={{0,24},{4,28},{8,0},{12,4},{16,8},{20,12},{24,16},{28,20},{1,25},{... | collective-permute-start | bytes 491528 | tf_op jit(solution)/shard_map/ppermute | solution.py:415
  189.2 24.9 %collective-permute-start.22 = (bf16[160,512]{1,0:T(8,128)(2,1)S(1)}, bf16[160,512]{1,0:T(8,128)(2,1)S(1)}, u32[]{:S(2)}, u32[]{:S(2)}) collective-permute-start(bf16[160,512]{1,0:T(8,128)(2,1)S(1)} %get-tuple-element.155), channel_id=1, source_target_pairs={{0,28},{4,0},{8,4},{12,8},{16,12},{20,16},{24,20},{28,24},{1,29},{... | collective-permute-start | bytes 491528 | tf_op jit(solution)/shard_map/ppermute | solution.py:415
  218.1 6.6 %collective-permute-start.23 = (bf16[2,128,512]{2,1,0:T(8,128)(2,1)S(1)}, bf16[2,128,512]{2,1,0:T(8,128)(2,1)S(1)}, u32[]{:S(2)}, u32[]{:S(2)}) collective-permute-start(bf16[2,128,512]{2,1,0:T(8,128)(2,1)S(1)} %get-tuple-element.158), channel_id=1, source_target_pairs={{0,1},{1,2},{2,3},{3,0},{4,5},{5,6},{6,7},{7,4},{8,9},{9,10},{10,1... | collective-permute-start | bytes 786440 | tf_op jit(solution)/shard_map/ppermute | solution.py:415
  219.2 12.4 %collective-permute-start.24 = (bf16[2,128,512]{2,1,0:T(8,128)(2,1)S(1)}, bf16[2,128,512]{2,1,0:T(8,128)(2,1)S(1)}, u32[]{:S(2)}, u32[]{:S(2)}) collective-permute-start(bf16[2,128,512]{2,1,0:T(8,128)(2,1)S(1)} %get-tuple-element.159), channel_id=1, source_target_pairs={{0,2},{1,3},{2,0},{3,1},{4,6},{5,7},{6,4},{7,5},{8,10},{9,11},{10,... | collective-permute-start | bytes 786440 | tf_op jit(solution)/shard_map/ppermute | solution.py:415
  220.0 12.2 %collective-permute-start.25 = (bf16[2,128,512]{2,1,0:T(8,128)(2,1)S(1)}, bf16[2,128,512]{2,1,0:T(8,128)(2,1)S(1)}, u32[]{:S(2)}, u32[]{:S(2)}) collective-permute-start(bf16[2,128,512]{2,1,0:T(8,128)(2,1)S(1)} %get-tuple-element.160), channel_id=1, source_target_pairs={{0,3},{1,0},{2,1},{3,2},{4,7},{5,4},{6,5},{7,6},{8,11},{9,8},{10,9... | collective-permute-start | bytes 786440 | tf_op jit(solution)/shard_map/ppermute | solution.py:415
  232.2 1.9 copy-start.1
